TPU v7x, 32 devices: a whole 2x2x4 slice. The times are simulated.
32 devices in a mesh: seq: 8 (over z, x), head: 4 (over y, core).
Axes of the slice: x: 2, y: 2, z: 4, core: 2. Of those that a mesh axis runs over, the one named last changes fastest.
Arguments:
- x_inputs: bfloat16 [65536, 1024], P('seq', 'head'), may hold values from -6 to 6
- x_in_proj: bfloat16 [65536, 128], P('seq'), may hold values from -0.5 to 0.5
- x_out_proj: bfloat16 [65536, 128], P('seq'), may hold values from -6 to 6
- x_log_decay: float32 [16, 65536], P('head', 'seq'), may hold values from -0.6 to 0
- x_step: float32 [16, 65536], P('head', 'seq'), may hold values from 0 to 0.5
- z_source: int32 [65536], P('seq'), may hold values from 0 to 65535, as said below
- z_in_proj: bfloat16 [65536, 128], P('seq'), may hold values from -0.5 to 0.5
- z_out_proj: bfloat16 [65536, 128], P('seq'), may hold values from -6 to 6
- z_log_decay: float32 [16, 65536], P('head', 'seq'), may hold values from -0.6 to 0
- z_step: float32 [16, 65536], P('head', 'seq'), may hold values from 0 to 0.5
- gate_branch: bfloat16 [65536, 1024], P('seq', 'head'), may hold values from -8 to 8
- norm_gain: float32 [1024], P('head'), may hold values from 0.1 to 1.9
- out_weight: bfloat16 [1024, 512], P('head'), may hold values from -0.1875 to 0.1875
Outputs:
- layer_out: bfloat16 [65536, 512], P(('seq', 'head'))
Inputs may be any that keep to these rules, and one draw needn't show every extreme that they name: z_source is a permutation; every block of 8192 consecutive z-order positions takes exactly 1024 tokens from each block of 8192 consecutive x-order tokens.
All inputs are finite; a program needn't handle non-finite values.
Results may differ from a plain program's by a relative error of at most 0.034.
Values may be sent and summed in bfloat16 or wider, within the bound.
A program may use at most 128 MiB of HBM per device.

v0:
```python
import jax
import jax.numpy as jnp
from jax import lax
from jax.sharding import PartitionSpec as P

BLOCK = 512


def shifted(value, axis, steps):
    count = lax.axis_size(axis)
    initial, last = (max(0, -steps), min(count, count - steps))
    return lax.ppermute(value, axis, [(source, source + steps) for source in range(initial, last)])


def local_blocks(inputs, b_mat, c_mat, log_decay, step):
    count = inputs.shape[0]
    blocks = count // BLOCK
    heads = log_decay.shape[0]
    width = inputs.shape[1]
    head_width = width // heads
    state = b_mat.shape[1]
    cum = jnp.cumsum(log_decay.reshape(heads, blocks, BLOCK), axis=2).transpose(1, 0, 2)
    totals = cum[:, :, -1]
    step_blocks = step.reshape(heads, blocks, BLOCK).transpose(1, 0, 2)
    u_blocks = inputs.reshape(blocks, BLOCK, heads, head_width)
    b_blocks = b_mat.reshape(blocks, BLOCK, state)
    c_blocks = c_mat.reshape(blocks, BLOCK, state)
    rows = lax.broadcasted_iota(jnp.int32, (BLOCK, BLOCK), 0)
    cols = lax.broadcasted_iota(jnp.int32, (BLOCK, BLOCK), 1)
    lower = rows >= cols

    def one_block(carry, pieces):
        u_blk, b_blk, c_blk, cum_blk, d_blk, tot_blk = pieces
        scores = jnp.dot(c_blk, b_blk.T, preferred_element_type=jnp.float32)
        diff = jnp.where(lower[None], cum_blk[:, :, None] - cum_blk[:, None, :], -jnp.inf)
        weights = (scores[None] * jnp.exp(diff) * d_blk[:, None, :]).astype(jnp.bfloat16)
        intra = jnp.einsum("hts,shp->thp", weights, u_blk, preferred_element_type=jnp.float32)
        scale = (jnp.exp(tot_blk[:, None] - cum_blk) * d_blk).T
        contrib = (u_blk * scale[:, :, None]).astype(jnp.bfloat16)
        state_add = jnp.einsum("shp,sn->hpn", contrib, b_blk, preferred_element_type=jnp.float32)
        updated = jnp.exp(tot_blk)[:, None, None] * carry + state_add
        return (updated, (intra, carry))

    start = jnp.zeros((heads, head_width, state), jnp.float32)
    final, (intra_all, local_in) = lax.scan(
        one_block, start, (u_blocks, b_blocks, c_blocks, cum, step_blocks, totals)
    )
    return (intra_all, local_in, final, cum, totals, c_blocks)


def incoming_state(device_decay, final):

    def relay(index, pair):
        received = shifted(pair[1].astype(jnp.bfloat16), "seq", 1).astype(jnp.float32)
        return (received, device_decay[:, None, None] * received + final)

    start, _ = lax.fori_loop(0, lax.axis_size("seq") - 1, relay, (jnp.zeros_like(final), final))
    return start


def ssd_scan(inputs, b_mat, c_mat, log_decay, step):
    intra_all, local_in, final, cum, totals, c_blocks = local_blocks(
        inputs, b_mat, c_mat, log_decay, step
    )
    device_decay = jnp.exp(jnp.sum(totals, axis=0))
    start = incoming_state(device_decay, final)
    before = jnp.cumsum(totals, axis=0) - totals
    carried = local_in + jnp.exp(before)[:, :, None, None] * start[None]
    inter = jnp.einsum(
        "bqn,bhpn->bqhp", c_blocks, carried.astype(jnp.bfloat16), preferred_element_type=jnp.float32
    )
    inter = inter * jnp.exp(cum).transpose(0, 2, 1)[:, :, :, None]
    return (intra_all + inter).astype(jnp.bfloat16).reshape(inputs.shape)


def body(
    x_inputs,
    x_in_proj,
    x_out_proj,
    x_log_decay,
    x_step,
    z_source,
    z_in_proj,
    z_out_proj,
    z_log_decay,
    z_step,
    gate_branch,
    norm_gain,
    out_weight,
):
    y_x = ssd_scan(x_inputs, x_in_proj, x_out_proj, x_log_decay, x_step)
    whole = lax.all_gather(y_x, "seq", axis=0, tiled=True)
    u_z = jnp.take(whole, z_source, axis=0)
    y_z = ssd_scan(u_z, z_in_proj, z_out_proj, z_log_decay, z_step)
    gated = y_z.astype(jnp.float32) * jax.nn.silu(gate_branch.astype(jnp.float32))
    squares = lax.psum(jnp.sum(gated * gated, axis=1).astype(jnp.bfloat16), "head").astype(
        jnp.float32
    )
    mean_square = squares / (gated.shape[1] * lax.axis_size("head"))
    normed = (gated * lax.rsqrt(mean_square[:, None] + 1e-05) * norm_gain).astype(jnp.bfloat16)
    return lax.psum_scatter(
        jnp.dot(normed, out_weight, preferred_element_type=jnp.float32).astype(jnp.bfloat16),
        "head",
        scatter_dimension=0,
        tiled=True,
    )


def solution(mesh):
    placed = (
        P("seq", "head"),
        P("seq", None),
        P("seq", None),
        P("head", "seq"),
        P("head", "seq"),
        P("seq"),
        P("seq", None),
        P("seq", None),
        P("head", "seq"),
        P("head", "seq"),
        P("seq", "head"),
        P("head"),
        P("head", None),
    )
    return jax.shard_map(
        body, mesh=mesh, in_specs=placed, out_specs=P(("seq", "head"), None), check_vma=False
    )
```

profile of v0, /device:TPU:0, one launch (start us, length us, event | category | flops | bytes accessed | tf_op | source)
XLA Modules:
  0.0 1317.6 jit_solution(11065249124684540339)
XLA Ops:
  7.6 4.6 reduce-window.16
  13.7 4.6 reduce-window.14
  19.0 12.9 reshape.159
  31.9 12.7 copy.53
  44.6 4.3 broadcast.45.clone
  49.2 107.4 %while.56 = (s32[]{:T(128)}, f32[4,64,128]{2,1,0:T(8,128)S(1)}, f32[16,512,4,64]{1,3,2,0:T(8,128)}, f32[16,4,64,128]{3,2,1,0:T(8,128)S(1)}, f32[16,4]{1,0:T(8,12...) while((s32[]{:T(128)}, f32[4,64,128]{2,1,0:T(8,128)S(1)}, ...), condition=%wide.region_3.4_spmd.clone, body=%wide.region_2.3_spmd.clone.sunk | while | flops 240914432 | bytes 4689120 | solution.py:45
  58.1 3.3 fusion.97
  84.9 3.3 fusion.97
  98.4 3.3 fusion.97
  111.8 3.3 fusion.97
  125.2 3.3 fusion.97
  138.7 3.3 fusion.97
  157.4 52.2 %while.54 = (s32[]{:T(128)}, f32[4,64,128]{2,1,0:T(8,128)}, bf16[4,64,128]{2,1,0:T(8,128)(2,1)S(1)}, f32[4]{0:T(128)S(1)}, f32[4,64,128]{2,1,0:T(8,128)S(1)}, /*index=5*/s32[]{:T(128)}) while((s32[]{:T(128)}, f32[4,64,128]{2,1,0:T(8,128)}, bf16[4,64,128]{2,1,0:T(8,128)(2,1)S(1)}, f32[4]{0:T(128)S(1)}, f32[4,64,128]{2,1,0:T(8,128)S(1)}, ...), condition=%wide.region_7.8_spmd, body=%wide.region_6.7_spmd.sunk | while | flops 131074 | bytes 655485 | solution.py:57
  157.4 4.8 collective-permute-start
  164.8 4.3 collective-permute-start
  171.6 4.3 collective-permute-start
  178.5 5.2 collective-permute-start
  186.3 5.2 collective-permute-start
  194.0 5.2 collective-permute-start
  202.3 4.8 collective-permute-start
  209.7 7.3 fusion.55
  217.0 12.6 copy.73
  229.6 12.7 reshape.160
  243.5 6.3 copy.68
  250.0 634.2 %all-gather.2.cloned.1.call-done = bf16[65536,256]{1,0:T(8,128)(2,1)} async-done(((bf16[8192,256]{1,0:T(8,128)(2,1)}), bf16[65536,256]{1,0:T(8,128)(2,1)}) %all-gather.2.cloned.1.call-update) | async-done | bytes 33554448 | tf_op jit(solution)/shard_map/all_gather | solution.py:92
  884.2 124.4 %gather_fusion = bf16[8192,256]{1,0:T(8,128)(2,1)} fusion(bf16[65536,256]{1,0:T(8,128)(2,1)} %all-gather.2.cloned.1.call-done, s32[8192]{0:T(1024)S(1)} %fusion.65), kind=kCustom, calls=%fused_computation | custom fusion | bytes 8421376 | tf_op jit(solution)/shard_map/jit(_take)/gather | solution.py:93
  1008.6 6.4 copy.60
  1015.0 4.0 copy.81
  1019.4 4.4 copy.62
  1023.8 4.3 broadcast.45
  1028.3 107.4 %while.57 = (s32[]{:T(128)}, f32[4,64,128]{2,1,0:T(8,128)S(1)}, f32[16,512,4,64]{1,3,2,0:T(8,128)}, f32[16,4,64,128]{3,2,1,0:T(8,128)S(1)}, f32[16,4]{1,0:T(8,12...) while((s32[]{:T(128)}, f32[4,64,128]{2,1,0:T(8,128)S(1)}, ...), condition=%wide.region_11.12_spmd.clone, body=%wide.region_10.11_spmd.clone.sunk | while | flops 240914432 | bytes 4689120 | solution.py:45
  1064.1 3.3 fusion.105
  1077.5 3.3 fusion.105
  1091.0 3.3 fusion.105
  1117.8 3.3 fusion.105
  1136.5 51.2 %while.55 = (s32[]{:T(128)}, f32[4,64,128]{2,1,0:T(8,128)}, bf16[4,64,128]{2,1,0:T(8,128)(2,1)S(1)}, f32[4]{0:T(128)S(1)}, f32[4,64,128]{2,1,0:T(8,128)S(1)}, /*index=5*/s32[]{:T(128)}) while((s32[]{:T(128)}, f32[4,64,128]{2,1,0:T(8,128)}, bf16[4,64,128]{2,1,0:T(8,128)(2,1)S(1)}, f32[4]{0:T(128)S(1)}, f32[4,64,128]{2,1,0:T(8,128)S(1)}, ...), condition=%wide.region_15.16_spmd, body=%wide.region_14.15_spmd.sunk | while | flops 131074 | bytes 655485 | solution.py:57
  1141.3 4.6 collective-permute-start.1
  1148.5 5.2 collective-permute-start.1
  1156.2 5.2 collective-permute-start.1
  1163.9 5.2 collective-permute-start.1
  1171.6 5.2 collective-permute-start.1
  1179.7 5.2 collective-permute-start.1
  1187.7 5.4 fusion.56
  1193.1 4.9 copy.67
  1197.9 8.3 copy.82
  1212.3 10.1 psum.7
  1222.4 12.2 convolution_convert_fusion
  1234.7 75.7 %reduce-scatter.2.cloned.1.call-done = bf16[2048,512]{1,0:T(8,128)(2,1)} async-done(((bf16[8192,512]{1,0:T(8,128)(2,1)}), bf16[2048,512]{1,0:T(8,128)(2,1)}) %reduce-scatter.2.cloned.1.call-update) | async-done | bytes 2097168 | tf_op jit(solution)/shard_map/reduce_scatter | solution.py:101
  (360 shorter events, 231.9 us)
Async XLA Ops:
  6.5 1215.9 %copy-start = (bf16[256,512]{1,0:T(8,128)(2,1)S(1)}, bf16[256,512]{1,0:T(8,128)(2,1)}, u32[]{:S(2)}) copy-start(bf16[256,512]{1,0:T(8,128)(2,1)} %param.33) | copy-start | bytes 786436
  6.5 877.6 %all-gather.2.cloned.1.call-start = ((), (), s32[]{:S(2)}) async-start(), calls=%async_computation.1 | async-start | bytes 37748736 | tf_op jit(solution)/shard_map/all_gather | solution.py:92
  157.4 6.7 collective-permute-start
  164.8 6.1 collective-permute-start
  171.6 6.2 collective-permute-start
  178.5 7.0 collective-permute-start
  186.3 7.0 collective-permute-start
  194.0 7.6 collective-permute-start
  202.3 6.7 collective-permute-start
  242.3 0.8 copy-start.3
  242.4 1068.0 %reduce-scatter.2.cloned.1.call-start = ((), (), s32[]{:S(2)}) async-start(), calls=%async_computation.2 | async-start | bytes 10485760 | tf_op jit(solution)/shard_map/reduce_scatter | solution.py:101
  1136.5 4.2 collective-permute-start.1
  1141.3 6.5 collective-permute-start.1
  1148.5 7.0 collective-permute-start.1
  1156.2 7.0 collective-permute-start.1
  1163.9 7.0 collective-permute-start.1
  1171.6 7.4 collective-permute-start.1
  1179.7 7.1 collective-permute-start.1
  1197.9 11.5 copy-start.2
  1206.2 3.2 copy-start.1
  1209.4 13.0 copy-start.4
Sparse Core Ops, SparseCore 0:
  242.5 641.6 all-gather.1
  1234.8 75.4 reduce-scatter.1
where the time goes:
time: 1330 us; the launch traced here: 1320 us
  waiting for transfers between devices  737 us (55%)
  local copies, waits for them, and re-layouts  228 us (17%)
  matrix products  209 us (16%)
  starting transfers between devices  66.7 us (5%)
  other arithmetic  50.3 us (4%)
  between operations  14.1 us (1%)
    all_gather x1, waiting for transfers between devices, body(): whole = lax.all_gather(y_x, 'seq', axis=0, tiled=True)  634 us
    gather x2, local copies, waits for them, and re-layouts, body(): u_z = jnp.take(whole, z_source, axis=0)  131 us
    dot_general x32, matrix products, one_block(): jnp.einsum('hts,shp->thp', weights, u_blk, preferred_element_type=jnp.flo...  105 us
    reduce_scatter x1, waiting for transfers between devices, body(): lax.psum_scatter(jnp.dot(normed, out_weight, preferred_element_type=jnp.f...  75.7 us
    ppermute x14, starting transfers between devices, shifted(): lax.ppermute(value, axis, [(source, source + steps) for source in range(i...  66.5 us
    dot_general x32, matrix products, one_block(): scores = jnp.dot(c_blk, b_blk.T, preferred_element_type=jnp.float32)  40.4 us
    unnamed x17, local copies, waits for them, and re-layouts  39.9 us
    dot_general x32, matrix products, one_block(): jnp.einsum('shp,sn->hpn', contrib, b_blk, preferred_element_type=jnp.floa...  38.6 us
  transfers between devices with their start and end apart: 16, of which 16 were waited for; matrix products, arithmetic and copies ran while one was open for 1% of the time, Pallas kernels for 0%

commit v1 on v0

v1 whole, which is shorter than its diff:
```python
import functools
import math

import jax
import jax.numpy as jnp
from jax import lax
from jax.experimental import pallas as pl
from jax.experimental.pallas import tpu as pltpu
from jax.sharding import PartitionSpec as P

CHUNK = 256
STEP = 1024
UNROLL = 32
VMEM = 56 * 1024 * 1024
LOG2E = math.log2(math.e)


def spread(columns, first, heads, width):
    head_width = width // heads
    rows = columns.shape[0]
    lanes = lax.broadcasted_iota(jnp.int32, (rows, width), 1)
    out = jnp.broadcast_to(columns[:, first : first + 1], (rows, width))
    for h in range(1, heads):
        column = jnp.broadcast_to(columns[:, first + h : first + h + 1], (rows, width))
        out = jnp.where(lanes >= h * head_width, column, out)
    return out


def add_state(total, u, b, columns, heads):
    width = u.shape[1]
    scale = spread(columns, 3 * heads, heads, width)
    contrib = (u.astype(jnp.float32) * scale).astype(jnp.bfloat16)
    total[...] += lax.dot_general(
        b, contrib, (((0,), (0,)), ((), ())), preferred_element_type=jnp.float32
    )


def final_kernel(heads, u_ref, b_ref, col_ref, out_ref, total):
    @pl.when(pl.program_id(0) == 0)
    def _():
        total[...] = jnp.zeros_like(total)

    add_state(total, u_ref[...], b_ref[...], col_ref[...], heads)
    out_ref[...] = total[...].astype(out_ref.dtype)


def place_kernel(heads, place_ref, recv_ref, b_ref, col_ref, out_ref, u_out, total, held, stage):
    step = pl.program_id(0)

    @pl.when(step == 0)
    def _():
        total[...] = jnp.zeros_like(total)

        def rows(i, _):
            base = pl.multiple_of(i * UNROLL, UNROLL)
            stage[...] = recv_ref[pl.ds(base, UNROLL), :].astype(jnp.float32)
            for r in range(UNROLL):
                held[pl.ds(place_ref[base + r], 1), :] = stage[r : r + 1, :]
            return 0

        lax.fori_loop(0, recv_ref.shape[0] // UNROLL, rows, 0)

    count = b_ref.shape[0]
    u = held[pl.ds(pl.multiple_of(step * count, count), count), :].astype(jnp.bfloat16)
    u_out[...] = u
    add_state(total, u, b_ref[...], col_ref[...], heads)
    out_ref[...] = total[...].astype(out_ref.dtype)


def chunk_result(heads, u, b, c, columns, rows, state):
    count, width = u.shape
    head_width = width // heads
    scores = lax.dot_general(c, b, (((1,), (1,)), ((), ())), preferred_element_type=jnp.float32)
    lower = lax.broadcasted_iota(jnp.int32, (count, count), 0) >= lax.broadcasted_iota(
        jnp.int32, (count, count), 1
    )
    lanes = lax.broadcasted_iota(jnp.int32, (count, width), 1)
    grow = spread(columns, 2 * heads, heads, width)
    y = grow * jnp.dot(c, state[...].astype(jnp.bfloat16), preferred_element_type=jnp.float32)
    weights, inputs = [], []
    for h in range(heads):
        factor = jnp.exp2(columns[:, h : h + 1] - rows[h : h + 1, :])
        weights.append(jnp.where(lower, scores * factor, 0.0).astype(jnp.bfloat16))
        mine = (lanes >= h * head_width) & (lanes < (h + 1) * head_width)
        inputs.append(jnp.where(mine, u, jnp.zeros_like(u)))
    y += jnp.dot(
        jnp.concatenate(weights, axis=1),
        jnp.concatenate(inputs, axis=0),
        preferred_element_type=jnp.float32,
    )
    scale = spread(columns, heads, heads, width)
    contrib = (u.astype(jnp.float32) * scale).astype(jnp.bfloat16)
    state[...] = grow[count - 1 : count, :] * state[...] + lax.dot_general(
        b, contrib, (((0,), (0,)), ((), ())), preferred_element_type=jnp.float32
    )
    return y


def scan_gather_kernel(
    heads, pick_ref, u_ref, b_ref, c_ref, col_ref, row_ref, start_ref, out_ref, state, held, stage
):
    step = pl.program_id(0)

    @pl.when(step == 0)
    def _():
        state[...] = start_ref[...]

    y = chunk_result(
        heads, u_ref[...], b_ref[...], c_ref[...], col_ref[...], row_ref[0], state
    )
    held[pl.ds(pl.multiple_of(step * CHUNK, CHUNK), CHUNK), :] = y

    @pl.when(step == pl.num_programs(0) - 1)
    def _():
        def rows(i, _):
            base = pl.multiple_of(i * UNROLL, UNROLL)
            for r in range(UNROLL):
                stage[r : r + 1, :] = held[pl.ds(pick_ref[base + r], 1), :]
            out_ref[pl.ds(base, UNROLL), :] = stage[...].astype(out_ref.dtype)
            return 0

        lax.fori_loop(0, out_ref.shape[0] // UNROLL, rows, 0)


def scan_gate_kernel(
    heads, u_ref, b_ref, c_ref, col_ref, row_ref, start_ref, gate_ref, out_ref, state
):
    @pl.when(pl.program_id(0) == 0)
    def _():
        state[...] = start_ref[...]

    y = chunk_result(
        heads, u_ref[...], b_ref[...], c_ref[...], col_ref[...], row_ref[0], state
    )
    gate = gate_ref[...].astype(jnp.float32)
    out_ref[...] = (y * gate / (1.0 + jnp.exp(-gate))).astype(out_ref.dtype)


def tail_kernel(g_ref, gain_ref, w_ref, out_ref):
    groups, rows, width = g_ref.shape
    square = jnp.zeros((rows, 1), jnp.float32)
    for k in range(groups):
        g = g_ref[k].astype(jnp.float32)
        square += jnp.sum(g * g, axis=1, keepdims=True)
    inverse = lax.rsqrt(square / (groups * width) + 1e-05)
    total = jnp.zeros(out_ref.shape, jnp.float32)
    for k in range(groups):
        normed = (g_ref[k].astype(jnp.float32) * inverse * gain_ref[k : k + 1, :]).astype(
            jnp.bfloat16
        )
        total += jnp.dot(normed, w_ref[k], preferred_element_type=jnp.float32)
    out_ref[...] = total.astype(out_ref.dtype)


def params():
    return pltpu.CompilerParams(vmem_limit_bytes=VMEM)


def by_row(rows, width):
    return pl.BlockSpec((rows, width), lambda i: (i, 0))


def whole(*shape):
    return pl.BlockSpec(shape, lambda i: (0,) * len(shape))


def smem():
    return pl.BlockSpec(memory_space=pltpu.SMEM)


def f32(*shape):
    return pltpu.VMEM(shape, jnp.float32)


def bf16(*shape):
    return jax.ShapeDtypeStruct(shape, jnp.bfloat16)


def decay_tables(log_decay, step):
    heads, count = log_decay.shape
    chunks = count // CHUNK
    ones = jnp.triu(jnp.ones((CHUNK, CHUNK), jnp.float32))
    g = log_decay.reshape(heads * chunks, CHUNK) * LOG2E
    cum = jnp.dot(g, ones, precision=lax.Precision.HIGHEST).reshape(heads, chunks, CHUNK)
    dt = step.reshape(heads, chunks, CHUNK)
    totals = cum[:, :, -1]
    after = lax.cumsum(totals, axis=1, reverse=True) - totals
    rest = totals[:, :, None] - cum
    columns = jnp.concatenate(
        [cum, jnp.exp2(rest) * dt, jnp.exp2(cum), jnp.exp2(rest + after[:, :, None]) * dt]
    )
    rows = (cum - jnp.log2(dt)).transpose(1, 0, 2)
    return columns.reshape(4 * heads, count).T, rows, jnp.sum(totals, axis=1)


def start_state(final, totals, width):
    me = lax.axis_index("seq")
    finals = lax.all_gather(final, "seq")
    count, heads = totals.shape
    place = jnp.arange(count)
    between = (place[None, :] > place[:, None]) & (place[None, :] < me)
    log = jnp.sum(jnp.where(between[:, :, None], totals[None], 0.0), axis=1)
    coef = jnp.where(place[:, None] < me, jnp.exp2(log), 0.0)
    coef = jnp.repeat(coef, width // heads, axis=1)
    return jnp.sum(coef[:, None, :] * finals.astype(jnp.float32), axis=0)


def body(
    x_inputs,
    x_in_proj,
    x_out_proj,
    x_log_decay,
    x_step,
    z_source,
    z_in_proj,
    z_out_proj,
    z_log_decay,
    z_step,
    gate_branch,
    norm_gain,
    out_weight,
):
    count, width = x_inputs.shape
    heads = x_log_decay.shape[0]
    state = x_in_proj.shape[1]
    peers = lax.axis_size("seq")
    groups = lax.axis_size("head")
    share = count // peers
    big = min(STEP, count)

    order, place = lax.sort((z_source, lax.iota(jnp.int32, count)), num_keys=1)
    pick = order.reshape(peers, share) - lax.iota(jnp.int32, peers)[:, None] * count
    pick = lax.all_to_all(pick, "seq", 0, 0).reshape(count)

    x_cols, x_rows, x_total = decay_tables(x_log_decay, x_step)
    z_cols, z_rows, z_total = decay_tables(z_log_decay, z_step)
    totals = lax.all_gather(jnp.stack([x_total, z_total]), "seq")
    weight = lax.all_gather(out_weight, "head")
    gain = lax.all_gather(norm_gain, "head")

    cols = x_cols.shape[1]
    chunk_specs = [
        by_row(CHUNK, width),
        by_row(CHUNK, state),
        by_row(CHUNK, state),
        by_row(CHUNK, cols),
        pl.BlockSpec((1, heads, CHUNK), lambda i: (i, 0, 0)),
        whole(state, width),
    ]

    x_final = pl.pallas_call(
        functools.partial(final_kernel, heads),
        out_shape=bf16(state, width),
        grid=(count // big,),
        in_specs=[by_row(big, width), by_row(big, state), by_row(big, cols)],
        out_specs=whole(state, width),
        scratch_shapes=[f32(state, width)],
        compiler_params=params(),
        name="x_final",
    )(x_inputs, x_in_proj, x_cols)
    x_start = start_state(x_final, totals[:, 0], width)
    sent = pl.pallas_call(
        functools.partial(scan_gather_kernel, heads),
        out_shape=bf16(count, width),
        grid=(count // CHUNK,),
        in_specs=[smem()] + chunk_specs,
        out_specs=whole(count, width),
        scratch_shapes=[f32(state, width), f32(count, width), f32(UNROLL, width)],
        compiler_params=params(),
        name="x_scan",
    )(pick, x_inputs, x_in_proj, x_out_proj, x_cols, x_rows, x_start)

    received = lax.all_to_all(sent.reshape(peers, share, width), "seq", 0, 0)
    received = received.reshape(count, width)

    z_final, u_z = pl.pallas_call(
        functools.partial(place_kernel, heads),
        out_shape=(bf16(state, width), bf16(count, width)),
        grid=(count // big,),
        in_specs=[smem(), whole(count, width), by_row(big, state), by_row(big, cols)],
        out_specs=(whole(state, width), by_row(big, width)),
        scratch_shapes=[f32(state, width), f32(count, width), f32(UNROLL, width)],
        compiler_params=params(),
        name="z_place",
    )(place, received, z_in_proj, z_cols)
    z_start = start_state(z_final, totals[:, 1], width)
    gated = pl.pallas_call(
        functools.partial(scan_gate_kernel, heads),
        out_shape=bf16(count, width),
        grid=(count // CHUNK,),
        in_specs=chunk_specs + [by_row(CHUNK, width)],
        out_specs=by_row(CHUNK, width),
        scratch_shapes=[f32(state, width)],
        compiler_params=params(),
        name="z_scan",
    )(u_z, z_in_proj, z_out_proj, z_cols, z_rows, z_start, gate_branch)

    mine = count // groups
    swapped = lax.all_to_all(gated.reshape(groups, mine, width), "head", 0, 0)
    model = out_weight.shape[1]
    tile = min(512, mine)
    return pl.pallas_call(
        tail_kernel,
        out_shape=bf16(mine, model),
        grid=(mine // tile,),
        in_specs=[
            pl.BlockSpec((groups, tile, width), lambda i: (0, i, 0)),
            whole(groups, width),
            whole(groups, width, model),
        ],
        out_specs=by_row(tile, model),
        compiler_params=params(),
        name="tail",
    )(swapped, gain, weight)


def solution(mesh):
    placed = (
        P("seq", "head"),
        P("seq", None),
        P("seq", None),
        P("head", "seq"),
        P("head", "seq"),
        P("seq"),
        P("seq", None),
        P("seq", None),
        P("head", "seq"),
        P("head", "seq"),
        P("seq", "head"),
        P("head"),
        P("head", None),
    )
    return jax.shard_map(
        body, mesh=mesh, in_specs=placed, out_specs=P(("seq", "head"), None), check_vma=False
    )
```

time: 1330 us -> 400 us (0.30)
  waiting for transfers between devices: 737 us -> 80 us
  local copies, waits for them, and re-layouts: 228 us -> 8.41 us
  matrix products: 209 us -> 0.77 us
  blocking collectives: 10.1 us -> 138 us
  Pallas kernels: 0 us -> 124 us
  starting transfers between devices: 66.7 us -> 17 us
  other arithmetic: 50.3 us -> 15.5 us
    all_gather x1, waiting for transfers between devices: 634 us -> 0.01 us  [body(): weight = lax.all_gather(out_weight, 'head')]
    dot_general x99 -> x2, matrix products: 209 us -> 0.77 us  [decay_tables(): jnp.dot(g, ones, precision=lax.Precision.HIGHEST)]
    all_gather x0 -> x4, blocking collectives: none -> 138 us  [the longest x2 63.2 us: start_state(): finals = lax.all_gather(final, 'seq')]
    gather x2 -> x0, local copies, waits for them, and re-layouts: 131 us -> none  [body(): u_z = jnp.take(whole, z_source, axis=0)]
    pallas_call x0 -> x5, Pallas kernels: none -> 124 us  [the longest x1 48.7 us: body(): pl.pallas_call(functools.partial(scan_gather_kernel, heads), out_shape=bf...]
    all_to_all x0 -> x3, waiting for transfers between devices: none -> 79.3 us  [the longest x1 79.3 us: body(): received = lax.all_to_all(sent.reshape(peers, share, width), 'seq', 0, 0)]
    reduce_scatter x1 -> x0, waiting for transfers between devices: 75.7 us -> none  [body(): lax.psum_scatter(jnp.dot(normed, out_weight, preferred_element_type=jnp.f...]
    ppermute x14 -> x0, starting transfers between devices: 66.5 us -> none  [shifted(): lax.ppermute(value, axis, [(source, source + steps) for source in range(i...]
  transfers between devices with their start and end apart: 16 -> 4, of which waited for: 16 -> 1; matrix products, arithmetic and copies ran while one was open for 1% -> 4% of each run, Pallas kernels for 0% -> 3%
where the time goes in v1:
time: 400 us; the launch traced here: 398 us
  blocking collectives  138 us (34%)
  Pallas kernels  124 us (31%)
  waiting for transfers between devices  80 us (20%)
  starting transfers between devices  17 us (4%)
  other arithmetic  15.5 us (4%)
  between operations  13.5 us (3%)
  local copies, waits for them, and re-layouts  8.41 us (2%)
    all_to_all x1, waiting for transfers between devices, body(): received = lax.all_to_all(sent.reshape(peers, share, width), 'seq', 0, 0)  79.3 us
    all_gather x2, blocking collectives, start_state(): finals = lax.all_gather(final, 'seq')  63.2 us
    all_gather x1, blocking collectives, body(): gain = lax.all_gather(norm_gain, 'head')  53.9 us
    pallas_call x1, Pallas kernels, body(): pl.pallas_call(functools.partial(scan_gather_kernel, heads), out_shape=bf...  48.7 us
    pallas_call x1, Pallas kernels, body(): pl.pallas_call(functools.partial(scan_gate_kernel, heads), out_shape=bf16...  31.3 us
    pallas_call x1, Pallas kernels, body(): pl.pallas_call(functools.partial(place_kernel, heads), out_shape=(bf16(st...  27.3 us
    all_gather x1, blocking collectives, body(): totals = lax.all_gather(jnp.stack([x_total, z_total]), 'seq')  21 us
    pallas_call x1, Pallas kernels, body(): pl.pallas_call(functools.partial(final_kernel, heads), out_shape=bf16(sta...  10.2 us
  transfers between devices with their start and end apart: 4, of which 1 were waited for; matrix products, arithmetic and copies ran while one was open for 4% of the time, Pallas kernels for 3%

profile of v1, /device:TPU:0, one launch (start us, length us, event | category | flops | bytes accessed | tf_op | source)
XLA Modules:
  0.0 397.6 jit_solution(12306265393106596822)
XLA Ops:
  6.5 7.5 %sort.15 = (s32[8192]{0:T(1024)S(1)}, s32[8192]{0:T(1024)}) sort(s32[8192]{0:T(1024)} %param.18, s32[8192]{0:T(1024)S(1)} %iota.51), dimensions={0}, to_apply=%region_0.0 | sort | flops 106496 | bytes 131072 | tf_op jit(solution)/shard_map/sort | solution.py:231
  14.0 0.7 broadcast_subtract_fusion
  14.7 7.3 %all-to-all-start = ((s32[8,1,1024]{2,1,0:T(1,128)}), s32[8,1,1024]{2,1,0:T(1,128)S(1)}, u32[]{:S(2)}, u32[]{:S(2)}) async-start(s32[8,1,1024]{2,1,0:T(1,128)} %broadcast_subtract_fusion), calls=%async_computation | async-start | bytes 65536 | tf_op jit(solution)/shard_map/all_to_all | solution.py:233
  22.0 0.9 broadcast_multiply_fusion.1
  22.9 0.4 fusion.4
  23.3 0.1 slice.16
  23.4 0.3 copy.110
  23.7 0.3 reduce_window_sum.16
  24.0 0.9 broadcast_multiply_fusion
  25.0 0.4 fusion.2
  25.4 0.1 slice.17
  25.5 0.3 reduce_window_sum.17
  25.8 0.2 slice_subtract_fusion
  26.0 21.0 %all-gather.5 = f32[8,2,4]{2,1,0:T(2,128)S(1)} all-gather(f32[1,2,4]{2,1,0:T(2,128)S(1)} %maximum_bitcast_fusion), channel_id=2, replica_groups=mesh['seq'=8,'head'=4] {'seq'}, dimensions={0}, use_global_device_ids=true | all-gather | bytes 288 | tf_op jit(solution)/shard_map/all_gather | solution.py:237
  47.0 0.1 copy.98
  47.0 0.1 copy.108
  47.1 0.1 select_reduce_fusion
  47.2 0.1 copy.99
  47.3 0.1 broadcast_in_dim.80
  47.4 0.1 mul.61
  47.5 0.3 copy.111
  47.8 1.8 exponential_multiply_fusion.3
  49.6 0.1 pad_maximum_fusion
  49.7 2.6 copy.112
  52.3 10.2 %x_final.1 = bf16[128,256]{1,0:T(8,128)(2,1)} custom-call(bf16[8192,256]{1,0:T(8,128)(2,1)} %u_ref.3, bf16[8192,128]{1,0:T(8,128)(2,1)} %b_ref.5, f32[8192,16]{1,0:T(8,128)} %bitcast.51), custom_call_target="tpu_custom_call" | custom-call | tf_op jit(solution)/shard_map/x_final/pallas_call | solution.py:251
  62.5 31.7 %all-gather.1 = bf16[1024,256]{1,0:T(8,128)(2,1)S(1)} all-gather(bf16[128,256]{1,0:T(8,128)(2,1)} %x_final.1), channel_id=3, replica_groups=mesh['seq'=8,'head'=4] {'seq'}, dimensions={0}, use_global_device_ids=true | all-gather | bytes 589824 | tf_op jit(solution)/shard_map/all_gather | solution.py:198
  94.2 0.8 fusion.1.start_ref
  95.0 0.6 copy-done
  95.6 48.7 %x_scan.1 = bf16[8192,256]{1,0:T(8,128)(2,1)} custom-call(s32[8192]{0:T(1024)} %bitcast.58, bf16[8192,256]{1,0:T(8,128)(2,1)} %u_ref.3, bf16[8192,128]{1,0:T(8,128)(2,1)} %b_ref.5, bf16[8192,128]{1,0:T(8,128)(2,1)} %c_ref.2, f32[8192,16]{1,0:T(8,128)} %bitcast.52, f32[32,4,256]{2,1,0:T(4,128)} %get-tuple-element.20.row_ref, f32[128,256]{1,0:T(8,128)} %fusion.1.start_ref), custom_call_target="tpu_custom_call" | custom-call | tf_op jit(solution)/shard_map/x_scan/pallas_call | solution.py:262
  144.3 4.7 %all-to-all-start.1 = ((bf16[8,1024,256]{2,1,0:T(8,128)(2,1)}), bf16[8,1024,256]{2,1,0:T(8,128)(2,1)}, u32[]{:S(2)}, u32[]{:S(2)}) async-start(bf16[8,1024,256]{2,1,0:T(8,128)(2,1)} %bitcast.53), calls=%async_computation.1 | async-start | bytes 8388608 | tf_op jit(solution)/shard_map/all_to_all | solution.py:273
  149.0 0.3 copy.114
  149.3 0.3 copy.115
  149.6 0.9 exponential_multiply_fusion.1
  150.5 0.1 pad_maximum_fusion.1
  150.7 2.6 copy.116
  153.3 0.1 copy.109
  153.3 0.1 broadcast_in_dim.83
  153.4 0.1 mul.66
  153.5 79.3 %all-to-all-done.1 = bf16[8,1024,256]{2,1,0:T(8,128)(2,1)} async-done(((bf16[8,1024,256]{2,1,0:T(8,128)(2,1)}), bf16[8,1024,256]{2,1,0:T(8,128)(2,1)}, u32[]{:S(2)}, u32[]{:S(2)}) %all-to-all-start.1) | async-done | bytes 4194336 | tf_op jit(solution)/shard_map/all_to_all | solution.py:273
  232.8 27.3 %z_place.1 = (bf16[128,256]{1,0:T(8,128)(2,1)}, bf16[8192,256]{1,0:T(8,128)(2,1)}) custom-call(s32[8192]{0:T(1024)} %get-tuple-element.9.place_ref, bf16[8192,256]{1,0:T(8,128)(2,1)} %bitcast.16.recv_ref, bf16[8192,128]{1,0:T(8,128)(2,1)} %b_ref.7, f32[8192,16]{1,0:T(8,128)} %bitcast.49), custom_call_target="tpu_custom_call" | custom-call | tf_op jit(solution)/shard_map/z_place/pallas_call | solution.py:276
  260.2 31.6 %all-gather.2 = bf16[1024,256]{1,0:T(8,128)(2,1)S(1)} all-gather(bf16[128,256]{1,0:T(8,128)(2,1)} %get-tuple-element.12), channel_id=4, replica_groups=mesh['seq'=8,'head'=4] {'seq'}, dimensions={0}, use_global_device_ids=true | all-gather | bytes 589824 | tf_op jit(solution)/shard_map/all_gather | solution.py:198
  291.7 0.8 fusion.start_ref
  292.5 31.3 %z_scan.1 = bf16[8192,256]{1,0:T(8,128)(2,1)} custom-call(bf16[8192,256]{1,0:T(8,128)(2,1)} %get-tuple-element.11.u_ref, bf16[8192,128]{1,0:T(8,128)(2,1)} %b_ref.7, bf16[8192,128]{1,0:T(8,128)(2,1)} %c_ref.3, f32[8192,16]{1,0:T(8,128)} %bitcast.50, f32[32,4,256]{2,1,0:T(4,128)} %get-tuple-element.19.row_ref, f32[128,256]{1,0:T(8,128)} %fusion.start_ref, ...), custom_call_target="tpu_custom_call" | custom-call | tf_op jit(solution)/shard_map/z_scan/pallas_call | solution.py:287
  323.8 5.0 %all-to-all-start.2 = ((bf16[4,2048,256]{2,1,0:T(8,128)(2,1)}), bf16[4,2048,256]{2,1,0:T(8,128)(2,1)}, u32[]{:S(2)}, u32[]{:S(2)}) async-start(bf16[4,2048,256]{2,1,0:T(8,128)(2,1)} %bitcast.54), calls=%async_computation.2 | async-start | bytes 8388608 | tf_op jit(solution)/shard_map/all_to_all | solution.py:299
  328.9 0.7 all-gather.9.cloned.1.call-update
  329.6 53.9 %all-gather.6 = f32[4,1,256]{2,1,0:T(1,128)S(1)} all-gather(f32[1,1,256]{2,1,0:T(1,128)S(1)} %bitcast.73), channel_id=5, replica_groups=mesh['seq'=8,'head'=4] {'head'}, dimensions={0}, use_global_device_ids=true | all-gather | bytes 5120 | tf_op jit(solution)/shard_map/all_gather | solution.py:239
  383.5 0.6 copy.140
  384.1 6.6 %tail.1 = bf16[2048,512]{1,0:T(8,128)(2,1)} custom-call(bf16[4,2048,256]{2,1,0:T(8,128)(2,1)} %all-to-all-done.2.g_ref, f32[4,256]{1,0:T(4,128)} %bitcast.68, bf16[4,256,512]{2,1,0:T(8,128)(2,1)} %bitcast.57), custom_call_target="tpu_custom_call" | custom-call | tf_op jit(solution)/shard_map/tail/pallas_call | solution.py:302
  (17 shorter events, 0.1 us)
Async XLA Ops:
  14.7 80.2 %all-to-all-start = ((s32[8,1,1024]{2,1,0:T(1,128)}), s32[8,1,1024]{2,1,0:T(1,128)S(1)}, u32[]{:S(2)}, u32[]{:S(2)}) async-start(s32[8,1,1024]{2,1,0:T(1,128)} %broadcast_subtract_fusion), calls=%async_computation | async-start | bytes 65536 | tf_op jit(solution)/shard_map/all_to_all | solution.py:233
  95.0 0.6 copy-start
  144.3 5.3 %copy-start.1 = (f32[4,8192]{1,0:T(4,128)S(1)}, f32[4,8192]{1,0:T(4,128)}, u32[]{:S(2)}) copy-start(f32[4,8192]{1,0:T(4,128)} %param.22) | copy-start | bytes 393220
  144.3 88.5 %all-to-all-start.1 = ((bf16[8,1024,256]{2,1,0:T(8,128)(2,1)}), bf16[8,1024,256]{2,1,0:T(8,128)(2,1)}, u32[]{:S(2)}, u32[]{:S(2)}) async-start(bf16[8,1024,256]{2,1,0:T(8,128)(2,1)} %bitcast.53), calls=%async_computation.1 | async-start | bytes 8388608 | tf_op jit(solution)/shard_map/all_to_all | solution.py:273
  323.8 5.7 %copy-start.2 = (f32[256]{0:T(256)S(1)}, f32[256]{0:T(256)}, u32[]{:S(2)}) copy-start(f32[256]{0:T(256)} %param.24) | copy-start | bytes 3076
  323.8 60.3 %all-to-all-start.2 = ((bf16[4,2048,256]{2,1,0:T(8,128)(2,1)}), bf16[4,2048,256]{2,1,0:T(8,128)(2,1)}, u32[]{:S(2)}, u32[]{:S(2)}) async-start(bf16[4,2048,256]{2,1,0:T(8,128)(2,1)} %bitcast.54), calls=%async_computation.2 | async-start | bytes 8388608 | tf_op jit(solution)/shard_map/all_to_all | solution.py:299
  328.8 55.3 %all-gather.9.cloned.1.call-start = ((), (), s32[]{:S(2)}) async-start(), calls=%async_computation.3 | async-start | bytes 1310720 | tf_op jit(solution)/shard_map/all_gather | solution.py:238
Sparse Core Ops, SparseCore 0:
  331.2 21.8 all-gather.8

commit v2 on v1

v2 whole, which is shorter than its diff:
```python
import functools
import math

import jax
import jax.numpy as jnp
from jax import lax
from jax.experimental import pallas as pl
from jax.experimental.pallas import tpu as pltpu
from jax.sharding import PartitionSpec as P

CHUNK = 256
STEP = 1024
UNROLL = 32
VMEM = 56 * 1024 * 1024
LOG2E = math.log2(math.e)


def spread(columns, first, heads, width):
    head_width = width // heads
    rows = columns.shape[0]
    lanes = lax.broadcasted_iota(jnp.int32, (rows, width), 1)
    out = jnp.broadcast_to(columns[:, first : first + 1], (rows, width))
    for h in range(1, heads):
        column = jnp.broadcast_to(columns[:, first + h : first + h + 1], (rows, width))
        out = jnp.where(lanes >= h * head_width, column, out)
    return out


def add_state(total, u, b, columns, heads, first, mine):
    width = u.shape[1]
    scale = spread(columns, 3 * heads + first, mine, width)
    contrib = (u.astype(jnp.float32) * scale).astype(jnp.bfloat16)
    total[...] += lax.dot_general(
        b, contrib, (((0,), (0,)), ((), ())), preferred_element_type=jnp.float32
    )


def final_kernel(heads, first, mine, u_ref, b_ref, col_ref, out_ref, total):
    @pl.when(pl.program_id(0) == 0)
    def _():
        total[...] = jnp.zeros_like(total)

    add_state(total, u_ref[...], b_ref[...], col_ref[...], heads, first, mine)
    out_ref[...] = total[...].astype(out_ref.dtype)


def place_kernel(
    heads, first, mine, place_ref, recv_ref, b_ref, col_ref, out_ref, u_out, total, held, stage
):
    step = pl.program_id(0)

    @pl.when(step == 0)
    def _():
        total[...] = jnp.zeros_like(total)

        def rows(i, _):
            base = pl.multiple_of(i * UNROLL, UNROLL)
            stage[...] = recv_ref[pl.ds(base, UNROLL), :].astype(jnp.float32)
            for r in range(UNROLL):
                held[pl.ds(place_ref[base + r], 1), :] = stage[r : r + 1, :]
            return 0

        lax.fori_loop(0, recv_ref.shape[0] // UNROLL, rows, 0)

    count = b_ref.shape[0]
    u = held[pl.ds(pl.multiple_of(step * count, count), count), :].astype(jnp.bfloat16)
    u_out[...] = u
    add_state(total, u, b_ref[...], col_ref[...], heads, first, mine)
    out_ref[...] = total[...].astype(out_ref.dtype)


def chunk_result(heads, first, mine, u, b, c, columns, rows, state):
    count, width = u.shape
    head_width = width // mine
    scores = lax.dot_general(c, b, (((1,), (1,)), ((), ())), preferred_element_type=jnp.float32)
    lower = lax.broadcasted_iota(jnp.int32, (count, count), 0) >= lax.broadcasted_iota(
        jnp.int32, (count, count), 1
    )
    lanes = lax.broadcasted_iota(jnp.int32, (count, width), 1)
    grow = spread(columns, 2 * heads + first, mine, width)
    y = grow * jnp.dot(c, state[...].astype(jnp.bfloat16), preferred_element_type=jnp.float32)
    weights, inputs = [], []
    for h in range(mine):
        at = first + h
        factor = jnp.exp2(columns[:, at : at + 1] - rows[at : at + 1, :])
        weights.append(jnp.where(lower, scores * factor, 0.0).astype(jnp.bfloat16))
        own = (lanes >= h * head_width) & (lanes < (h + 1) * head_width)
        inputs.append(jnp.where(own, u, jnp.zeros_like(u)))
    y += jnp.dot(
        jnp.concatenate(weights, axis=1),
        jnp.concatenate(inputs, axis=0),
        preferred_element_type=jnp.float32,
    )
    scale = spread(columns, heads + first, mine, width)
    contrib = (u.astype(jnp.float32) * scale).astype(jnp.bfloat16)
    state[...] = grow[count - 1 : count, :] * state[...] + lax.dot_general(
        b, contrib, (((0,), (0,)), ((), ())), preferred_element_type=jnp.float32
    )
    return y


def scan_gather_kernel(
    heads,
    first,
    mine,
    pick_ref,
    u_ref,
    b_ref,
    c_ref,
    col_ref,
    row_ref,
    start_ref,
    out_ref,
    state,
    held,
    stage,
):
    step = pl.program_id(0)

    @pl.when(step == 0)
    def _():
        state[...] = start_ref[...]

    y = chunk_result(
        heads, first, mine, u_ref[...], b_ref[...], c_ref[...], col_ref[...], row_ref[0], state
    )
    held[pl.ds(pl.multiple_of(step * CHUNK, CHUNK), CHUNK), :] = y

    @pl.when(step == pl.num_programs(0) - 1)
    def _():
        def rows(i, _):
            base = pl.multiple_of(i * UNROLL, UNROLL)
            for r in range(UNROLL):
                stage[r : r + 1, :] = held[pl.ds(pick_ref[base + r], 1), :]
            out_ref[pl.ds(base, UNROLL), :] = stage[...].astype(out_ref.dtype)
            return 0

        lax.fori_loop(0, out_ref.shape[0] // UNROLL, rows, 0)


def scan_gate_kernel(
    heads, first, mine, u_ref, b_ref, c_ref, col_ref, row_ref, start_ref, gate_ref, out_ref, state
):
    @pl.when(pl.program_id(0) == 0)
    def _():
        state[...] = start_ref[...]

    y = chunk_result(
        heads, first, mine, u_ref[...], b_ref[...], c_ref[...], col_ref[...], row_ref[0], state
    )
    gate = gate_ref[...].astype(jnp.float32)
    out_ref[...] = (y * gate / (1.0 + jnp.exp(-gate))).astype(out_ref.dtype)


def tail_kernel(parts, *refs):
    w_ref, out_ref = refs[parts:]
    groups, rows, width = refs[0].shape
    square = jnp.zeros((rows, 1), jnp.float32)
    total = jnp.zeros(out_ref.shape, jnp.float32)
    for p in range(parts):
        for k in range(groups):
            sent = refs[p][k]
            g = sent.astype(jnp.float32)
            square += jnp.sum(g * g, axis=1, keepdims=True)
            total += jnp.dot(
                sent, w_ref[k, p * width : (p + 1) * width, :], preferred_element_type=jnp.float32
            )
    inverse = lax.rsqrt(square / (parts * groups * width) + 1e-05)
    out_ref[...] = (total * inverse).astype(out_ref.dtype)


def after(value, *others):
    return lax.optimization_barrier((value,) + others)[0]


def to_all(value, axis):
    count = lax.axis_size(axis)
    return lax.all_to_all(jnp.broadcast_to(value, (count,) + value.shape), axis, 0, 0)


def params():
    return pltpu.CompilerParams(vmem_limit_bytes=VMEM)


def cost(flops, moved):
    return pl.CostEstimate(flops=flops, bytes_accessed=moved, transcendentals=0)


def by_row(rows, width, at=0):
    return pl.BlockSpec((rows, width), lambda i: (i, at))


def whole(*shape):
    return pl.BlockSpec(shape, lambda i: (0,) * len(shape))


def smem():
    return pl.BlockSpec(memory_space=pltpu.SMEM)


def f32(*shape):
    return pltpu.VMEM(shape, jnp.float32)


def bf16(*shape):
    return jax.ShapeDtypeStruct(shape, jnp.bfloat16)


def decay_tables(log_decay, step):
    heads, count = log_decay.shape
    chunks = count // CHUNK
    ones = jnp.triu(jnp.ones((CHUNK, CHUNK), jnp.float32))
    g = log_decay.reshape(heads * chunks, CHUNK) * LOG2E
    cum = jnp.dot(g, ones, precision=lax.Precision.HIGHEST).reshape(heads, chunks, CHUNK)
    dt = step.reshape(heads, chunks, CHUNK)
    totals = cum[:, :, -1]
    after = lax.cumsum(totals, axis=1, reverse=True) - totals
    rest = totals[:, :, None] - cum
    columns = jnp.concatenate(
        [cum, jnp.exp2(rest) * dt, jnp.exp2(cum), jnp.exp2(rest + after[:, :, None]) * dt]
    )
    rows = (cum - jnp.log2(dt)).transpose(1, 0, 2)
    return columns.reshape(4 * heads, count).T, rows, jnp.sum(totals, axis=1)


def start_state(final, totals, width):
    me = lax.axis_index("seq")
    finals = to_all(final, "seq")
    count, heads = totals.shape
    place = jnp.arange(count)
    between = (place[None, :] > place[:, None]) & (place[None, :] < me)
    log = jnp.sum(jnp.where(between[:, :, None], totals[None], 0.0), axis=1)
    coef = jnp.where(place[:, None] < me, jnp.exp2(log), 0.0)
    coef = jnp.repeat(coef, width // heads, axis=1)
    return jnp.sum(coef[:, None, :] * finals.astype(jnp.float32), axis=0)


def body(
    x_inputs,
    x_in_proj,
    x_out_proj,
    x_log_decay,
    x_step,
    z_source,
    z_in_proj,
    z_out_proj,
    z_log_decay,
    z_step,
    gate_branch,
    norm_gain,
    out_weight,
):
    count, width = x_inputs.shape
    heads = x_log_decay.shape[0]
    state = x_in_proj.shape[1]
    peers = lax.axis_size("seq")
    groups = lax.axis_size("head")
    share = count // peers
    big = min(STEP, count)

    order, place = lax.sort((z_source, lax.iota(jnp.int32, count)), num_keys=1)
    pick = order.reshape(peers, share) - lax.iota(jnp.int32, peers)[:, None] * count
    pick = lax.all_to_all(pick, "seq", 0, 0).reshape(count)

    x_cols, x_rows, x_total = decay_tables(x_log_decay, x_step)
    z_cols, z_rows, z_total = decay_tables(z_log_decay, z_step)
    totals = to_all(jnp.stack([x_total, z_total]), "seq")
    scaled = (out_weight.astype(jnp.float32) * norm_gain[:, None]).astype(jnp.bfloat16)
    weight = to_all(scaled, "head")

    parts = 2 if width % 256 == 0 and heads % 2 == 0 else 1
    own = heads // parts
    part = width // parts
    cols = x_cols.shape[1]
    moved = 64 * count * part

    def chunk_specs(u_at):
        return [
            by_row(CHUNK, part, u_at),
            by_row(CHUNK, state),
            by_row(CHUNK, state),
            by_row(CHUNK, cols),
            pl.BlockSpec((1, heads, CHUNK), lambda i: (i, 0, 0)),
            pl.BlockSpec((state, part), lambda i: (0, u_at)),
        ]

    x_final = pl.pallas_call(
        functools.partial(final_kernel, heads, 0, heads),
        out_shape=bf16(state, width),
        grid=(count // big,),
        in_specs=[by_row(big, width), by_row(big, state), by_row(big, cols)],
        out_specs=whole(state, width),
        scratch_shapes=[f32(state, width)],
        compiler_params=params(),
        name="x_final",
    )(x_inputs, x_in_proj, x_cols)
    x_start = start_state(x_final, totals[:, 0], width)

    received, done = [], []
    for p in range(parts):
        sent = pl.pallas_call(
            functools.partial(scan_gather_kernel, heads, p * own, own),
            out_shape=bf16(count, part),
            grid=(count // CHUNK,),
            in_specs=[smem()] + chunk_specs(p),
            out_specs=whole(count, part),
            scratch_shapes=[f32(state, part), f32(count, part), f32(UNROLL, part)],
            compiler_params=params(),
            cost_estimate=cost(0, moved),
            name="x_scan_%d" % p,
        )(pick, x_inputs, x_in_proj, x_out_proj, x_cols, x_rows, after(x_start, *done))
        done.append(sent)
        received.append(lax.all_to_all(sent.reshape(peers, share, part), "seq", 0, 0))

    mine = count // groups
    swapped = []
    done.append(weight)
    for p in range(parts):
        arrived = after(received[p], *done).reshape(count, part)
        z_final, u_z = pl.pallas_call(
            functools.partial(place_kernel, heads, p * own, own),
            out_shape=(bf16(state, part), bf16(count, part)),
            grid=(count // big,),
            in_specs=[smem(), whole(count, part), by_row(big, state), by_row(big, cols)],
            out_specs=(whole(state, part), by_row(big, part)),
            scratch_shapes=[f32(state, part), f32(count, part), f32(UNROLL, part)],
            compiler_params=params(),
            cost_estimate=cost(0, moved // 2),
            name="z_place_%d" % p,
        )(place, arrived, z_in_proj, z_cols)
        z_start = start_state(z_final, totals[:, 1, p * own : (p + 1) * own], part)
        gated = pl.pallas_call(
            functools.partial(scan_gate_kernel, heads, p * own, own),
            out_shape=bf16(count, part),
            grid=(count // CHUNK,),
            in_specs=chunk_specs(0) + [by_row(CHUNK, part, p)],
            out_specs=by_row(CHUNK, part),
            scratch_shapes=[f32(state, part)],
            compiler_params=params(),
            cost_estimate=cost(0, moved),
            name="z_scan_%d" % p,
        )(u_z, z_in_proj, z_out_proj, z_cols, z_rows, z_start, gate_branch)
        done = [gated]
        swapped.append(lax.all_to_all(gated.reshape(groups, mine, part), "head", 0, 0))

    model = out_weight.shape[1]
    tile = min(512, mine)
    return pl.pallas_call(
        functools.partial(tail_kernel, parts),
        out_shape=bf16(mine, model),
        grid=(mine // tile,),
        in_specs=[pl.BlockSpec((groups, tile, part), lambda i: (0, i, 0))] * parts
        + [whole(groups, width, model)],
        out_specs=by_row(tile, model),
        compiler_params=params(),
        name="tail",
    )(*swapped, weight)


def solution(mesh):
    placed = (
        P("seq", "head"),
        P("seq", None),
        P("seq", None),
        P("head", "seq"),
        P("head", "seq"),
        P("seq"),
        P("seq", None),
        P("seq", None),
        P("head", "seq"),
        P("head", "seq"),
        P("seq", "head"),
        P("head"),
        P("head", None),
    )
    return jax.shard_map(
        body, mesh=mesh, in_specs=placed, out_specs=P(("seq", "head"), None), check_vma=False
    )
```

time: 400 us -> 342 us (0.85)
  blocking collectives: 138 us -> 55.2 us
  Pallas kernels: 124 us -> 175 us
  waiting for transfers between devices: 80 us -> 42.8 us
  starting transfers between devices: 17 us -> 33.8 us
  between operations: 13.5 us -> 0.16 us
  local copies, waits for them, and re-layouts: 8.41 us -> 16.2 us
    all_gather x4 -> x0, blocking collectives: 138 us -> none  [the longest x2 63.2 us: start_state(): finals = lax.all_gather(final, 'seq')]
    all_to_all x0 -> x3, blocking collectives: none -> 55.2 us  [the longest x1 30.2 us: body(): lax.all_to_all(gated.reshape(groups, mine, part), 'head', 0, 0)]
    pallas_call x5 -> x8, Pallas kernels: 124 us -> 175 us  [the longest x2 71 us: body(): pl.pallas_call(functools.partial(scan_gather_kernel, heads, p * own, own)...]
    all_to_all x2 -> x6, waiting for transfers between devices: 79.3 us -> 42.8 us  [the longest x2 29.5 us: body(): lax.all_to_all(sent.reshape(peers, share, part), 'seq', 0, 0)]
    all_to_all x2 -> x6, starting transfers between devices: 9.72 us -> 27.9 us  [the longest x3 16.8 us: to_all(): lax.all_to_all(jnp.broadcast_to(value, (count,) + value.shape), axis, 0, 0)]
    broadcast_in_dim x0 -> x5, local copies, waits for them, and re-layouts: none -> 4.93 us  [to_all(): jnp.broadcast_to(value, (count,) + value.shape)]
  transfers between devices with their start and end apart: 4 -> 7, of which waited for: 1 -> 3; matrix products, arithmetic and copies ran while one was open for 4% -> 6% of each run, Pallas kernels for 3% -> 39%
where the time goes in v2:
time: 342 us; the launch traced here: 338 us
  Pallas kernels  175 us (51%)
  blocking collectives  55.2 us (16%)
  waiting for transfers between devices  42.8 us (13%)
  starting transfers between devices  33.8 us (10%)
  local copies, waits for them, and re-layouts  16.2 us (5%)
  other arithmetic  14.7 us (4%)
    pallas_call x2, Pallas kernels, body(): pl.pallas_call(functools.partial(scan_gather_kernel, heads, p * own, own)...  71 us
    pallas_call x2, Pallas kernels, body(): pl.pallas_call(functools.partial(scan_gate_kernel, heads, p * own, own),...  52.3 us
    pallas_call x2, Pallas kernels, body(): pl.pallas_call(functools.partial(place_kernel, heads, p * own, own), out_...  33.7 us
    all_to_all x1, blocking collectives, body(): lax.all_to_all(gated.reshape(groups, mine, part), 'head', 0, 0)  30.2 us
    all_to_all x2, waiting for transfers between devices, body(): lax.all_to_all(sent.reshape(peers, share, part), 'seq', 0, 0)  29.5 us
    all_to_all x2, blocking collectives, to_all(): lax.all_to_all(jnp.broadcast_to(value, (count,) + value.shape), axis, 0, 0)  25 us
    all_to_all x3, starting transfers between devices, to_all(): lax.all_to_all(jnp.broadcast_to(value, (count,) + value.shape), axis, 0, 0)  16.8 us
    all_to_all x3, waiting for transfers between devices, to_all(): lax.all_to_all(jnp.broadcast_to(value, (count,) + value.shape), axis, 0, 0)  13.2 us
  transfers between devices with their start and end apart: 7, of which 3 were waited for; matrix products, arithmetic and copies ran while one was open for 6% of the time, Pallas kernels for 39%

profile of v2, /device:TPU:0, one launch (start us, length us, event | category | flops | bytes accessed | tf_op | source)
XLA Modules:
  0.0 338.5 jit_solution(12808107442187257676)
XLA Ops:
  0.0 1.0 broadcast_multiply_fusion.1
  1.0 0.4 fusion.2
  1.4 0.9 broadcast_multiply_fusion
  2.4 0.4 fusion
  2.9 0.3 reduce_window_sum.16
  3.2 0.3 reduce_window_sum.17
  3.7 0.6 broadcast_in_dim.134
  4.3 7.3 %all-to-all-start.1 = ((f32[8,2,4]{2,1,0:T(2,128)}), f32[8,2,4]{2,1,0:T(2,128)S(1)}, u32[]{:S(2)}, u32[]{:S(2)}) async-start(f32[8,2,4]{2,1,0:T(2,128)} %broadcast_in_dim.134), calls=%async_computation.1 | async-start | bytes 16384 | tf_op jit(solution)/shard_map/all_to_all | solution.py:178
  11.6 0.3 copy.114
  11.9 0.3 copy.115
  12.2 6.8 %sort.15 = (s32[8192]{0:T(1024)S(1)}, s32[8192]{0:T(1024)}) sort(s32[8192]{0:T(1024)S(1)} %copy-done.8, s32[8192]{0:T(1024)S(1)} %iota.52), dimensions={0}, to_apply=%region_0.0 | sort | flops 106496 | bytes 131072 | tf_op jit(solution)/shard_map/sort | solution.py:261
  18.9 0.9 exponential_multiply_fusion.3
  19.8 0.7 broadcast_subtract_fusion
  20.5 6.0 %all-to-all-start = ((s32[8,1,1024]{2,1,0:T(1,128)}), s32[8,1,1024]{2,1,0:T(1,128)S(1)}, u32[]{:S(2)}, u32[]{:S(2)}) async-start(s32[8,1,1024]{2,1,0:T(1,128)} %broadcast_subtract_fusion), calls=%async_computation | async-start | bytes 65536 | tf_op jit(solution)/shard_map/all_to_all | solution.py:263
  26.7 2.6 copy.116
  29.3 10.2 %x_final.1 = bf16[128,256]{1,0:T(8,128)(2,1)} custom-call(bf16[8192,256]{1,0:T(8,128)(2,1)} %u_ref.5, bf16[8192,128]{1,0:T(8,128)(2,1)} %b_ref.9, f32[8192,16]{1,0:T(8,128)} %bitcast.46), custom_call_target="tpu_custom_call" | custom-call | tf_op jit(solution)/shard_map/x_final/pallas_call | solution.py:287
  39.5 1.7 broadcast_in_dim.140
  41.2 6.0 %all-to-all-start.2 = ((bf16[8,128,256]{2,1,0:T(8,128)(2,1)}), bf16[8,128,256]{2,1,0:T(8,128)(2,1)S(1)}, u32[]{:S(2)}, u32[]{:S(2)}) async-start(bf16[8,128,256]{2,1,0:T(8,128)(2,1)} %broadcast_in_dim.140), calls=%async_computation.2 | async-start | bytes 1048576 | tf_op jit(solution)/shard_map/all_to_all | solution.py:178
  47.3 13.2 %all-to-all-done.2 = bf16[8,128,256]{2,1,0:T(8,128)(2,1)S(1)} async-done(((bf16[8,128,256]{2,1,0:T(8,128)(2,1)}), bf16[8,128,256]{2,1,0:T(8,128)(2,1)S(1)}, u32[]{:S(2)}, u32[]{:S(2)}) %all-to-all-start.2) | async-done | bytes 524320 | tf_op jit(solution)/shard_map/all_to_all | solution.py:178
  60.6 1.1 broadcast_in_dim.141
  61.7 3.5 %all-to-all-start.4 = ((bf16[4,256,512]{2,1,0:T(8,128)(2,1)}), bf16[4,256,512]{2,1,0:T(8,128)(2,1)S(1)}, u32[]{:S(2)}, u32[]{:S(2)}) async-start(bf16[4,256,512]{2,1,0:T(8,128)(2,1)} %broadcast_in_dim.141), calls=%async_computation.4 | async-start | bytes 2097152 | tf_op jit(solution)/shard_map/all_to_all | solution.py:178
  65.7 0.8 multiply_reduce_fusion.start_ref
  66.4 35.5 %x_scan_0.1 = bf16[8192,128]{1,0:T(8,128)(2,1)} custom-call(s32[8192]{0:T(1024)} %bitcast.54, bf16[8192,256]{1,0:T(8,128)(2,1)} %u_ref.5, bf16[8192,128]{1,0:T(8,128)(2,1)} %b_ref.9, bf16[8192,128]{1,0:T(8,128)(2,1)} %c_ref.5, f32[8192,16]{1,0:T(8,128)} %bitcast.47, f32[32,4,256]{2,1,0:T(4,128)} %get-tuple-element.30.row_ref, ...), custom_call_target="tpu_custom_call" | custom-call | bytes 67108864 | tf_op jit(solution)/shard_map/x_scan_0/pallas_call | solution.py:301
  101.9 1.0 copy-done.3
  102.9 3.7 %all-to-all-start.3 = ((bf16[8,1024,128]{2,1,0:T(8,128)(2,1)}), bf16[8,1024,128]{2,1,0:T(8,128)(2,1)S(1)}, u32[]{:S(2)}, u32[]{:S(2)}) async-start(bf16[8,1024,128]{2,1,0:T(8,128)(2,1)} %bitcast.49), calls=%async_computation.3 | async-start | bytes 4194304 | tf_op jit(solution)/shard_map/all_to_all | solution.py:313
  106.6 0.3 copy.118
  106.9 0.3 copy.119
  107.2 0.9 exponential_multiply_fusion.1
  108.2 2.6 copy.120
  110.8 35.6 %x_scan_1.1 = bf16[8192,128]{1,0:T(8,128)(2,1)} custom-call(s32[8192]{0:T(1024)} %bitcast.55, bf16[8192,256]{1,0:T(8,128)(2,1)} %u_ref.5, bf16[8192,128]{1,0:T(8,128)(2,1)} %b_ref.9, bf16[8192,128]{1,0:T(8,128)(2,1)} %c_ref.5, f32[8192,16]{1,0:T(8,128)} %bitcast.48, f32[32,4,256]{2,1,0:T(4,128)} %get-tuple-element.30.row_ref, ...), custom_call_target="tpu_custom_call" | custom-call | bytes 67108864 | tf_op jit(solution)/shard_map/x_scan_1/pallas_call | solution.py:301
  146.3 9.2 %all-to-all-done.3 = bf16[8,1024,128]{2,1,0:T(8,128)(2,1)S(1)} async-done(((bf16[8,1024,128]{2,1,0:T(8,128)(2,1)}), bf16[8,1024,128]{2,1,0:T(8,128)(2,1)S(1)}, u32[]{:S(2)}, u32[]{:S(2)}) %all-to-all-start.3) | async-done | bytes 2097184 | tf_op jit(solution)/shard_map/all_to_all | solution.py:313
  155.6 1.3 copy-done.2
  156.9 16.9 %z_place_0.1 = (bf16[128,128]{1,0:T(8,128)(2,1)}, bf16[8192,128]{1,0:T(8,128)(2,1)}) custom-call(s32[8192]{0:T(1024)} %get-tuple-element.14.place_ref, bf16[8192,128]{1,0:T(8,128)(2,1)} %bitcast.51, bf16[8192,128]{1,0:T(8,128)(2,1)} %b_ref.13, f32[8192,16]{1,0:T(8,128)} %bitcast.42), custom_call_target="tpu_custom_call" | custom-call | bytes 33554432 | tf_op jit(solution)/shard_map/z_place_0/pallas_call | solution.py:320
  173.7 0.8 broadcast_in_dim.149
  174.5 12.6 %all_to_all.51 = bf16[8,128,128]{2,1,0:T(8,128)(2,1)S(1)} all-to-all(bf16[8,128,128]{2,1,0:T(8,128)(2,1)S(1)} %broadcast_in_dim.149), channel_id=1, replica_groups=mesh['seq'=8,'head'=4] {'seq'}, dimensions={0} | all-to-all | bytes 524288 | tf_op jit(solution)/shard_map/all_to_all | solution.py:178
  187.1 3.8 %all-to-all-start.7 = ((bf16[8,1024,128]{2,1,0:T(8,128)(2,1)}), bf16[8,1024,128]{2,1,0:T(8,128)(2,1)S(1)}, u32[]{:S(2)}, u32[]{:S(2)}) async-start(bf16[8,1024,128]{2,1,0:T(8,128)(2,1)} %bitcast.23), calls=%async_computation.7 | async-start | bytes 4194304 | tf_op jit(solution)/shard_map/all_to_all | solution.py:313
  191.4 0.7 multiply_reduce_fusion.2.start_ref
  192.1 26.2 %z_scan_0.1 = bf16[8192,128]{1,0:T(8,128)(2,1)} custom-call(bf16[8192,128]{1,0:T(8,128)(2,1)} %get-tuple-element.18.u_ref, bf16[8192,128]{1,0:T(8,128)(2,1)} %b_ref.13, bf16[8192,128]{1,0:T(8,128)(2,1)} %c_ref.7, f32[8192,16]{1,0:T(8,128)} %bitcast.43, f32[32,4,256]{2,1,0:T(4,128)} %get-tuple-element.29.row_ref, f32[128,128]{1,0:T(8,128)} %multiply_reduce_fusion.2.start_ref, ...), custom_call_target="tpu_custom_call" | custom-call | bytes 67108864 | tf_op jit(solution)/shard_map/z_scan_0/pallas_call | solution.py:332
  218.3 20.3 %all-to-all-done.7 = bf16[8,1024,128]{2,1,0:T(8,128)(2,1)S(1)} async-done(((bf16[8,1024,128]{2,1,0:T(8,128)(2,1)}), bf16[8,1024,128]{2,1,0:T(8,128)(2,1)S(1)}, u32[]{:S(2)}, u32[]{:S(2)}) %all-to-all-start.7) | async-done | bytes 2097184 | tf_op jit(solution)/shard_map/all_to_all | solution.py:313
  238.6 1.3 copy-done.1
  240.0 16.9 %z_place_1.1 = (bf16[128,128]{1,0:T(8,128)(2,1)}, bf16[8192,128]{1,0:T(8,128)(2,1)}) custom-call(s32[8192]{0:T(1024)} %get-tuple-element.14.place_ref, bf16[8192,128]{1,0:T(8,128)(2,1)} %bitcast.50, bf16[8192,128]{1,0:T(8,128)(2,1)} %b_ref.13, f32[8192,16]{1,0:T(8,128)} %bitcast.44), custom_call_target="tpu_custom_call" | custom-call | bytes 33554432 | tf_op jit(solution)/shard_map/z_place_1/pallas_call | solution.py:320
  256.8 0.8 broadcast_in_dim.153
  257.6 12.5 %all_to_all.52 = bf16[8,128,128]{2,1,0:T(8,128)(2,1)S(1)} all-to-all(bf16[8,128,128]{2,1,0:T(8,128)(2,1)S(1)} %broadcast_in_dim.153), channel_id=1, replica_groups=mesh['seq'=8,'head'=4] {'seq'}, dimensions={0} | all-to-all | bytes 524288 | tf_op jit(solution)/shard_map/all_to_all | solution.py:178
  270.1 3.6 %all-to-all-start.6 = ((bf16[4,2048,128]{2,1,0:T(8,128)(2,1)}), bf16[4,2048,128]{2,1,0:T(8,128)(2,1)S(1)}, u32[]{:S(2)}, u32[]{:S(2)}) async-start(bf16[4,2048,128]{2,1,0:T(8,128)(2,1)} %bitcast.52), calls=%async_computation.6 | async-start | bytes 4194304 | tf_op jit(solution)/shard_map/all_to_all | solution.py:344
  273.9 0.7 multiply_reduce_fusion.1.start_ref
  274.6 26.1 %z_scan_1.1 = bf16[8192,128]{1,0:T(8,128)(2,1)} custom-call(bf16[8192,128]{1,0:T(8,128)(2,1)} %get-tuple-element.21.u_ref, bf16[8192,128]{1,0:T(8,128)(2,1)} %b_ref.13, bf16[8192,128]{1,0:T(8,128)(2,1)} %c_ref.7, f32[8192,16]{1,0:T(8,128)} %bitcast.45, f32[32,4,256]{2,1,0:T(4,128)} %get-tuple-element.29.row_ref, f32[128,128]{1,0:T(8,128)} %multiply_reduce_fusion.1.start_ref, ...), custom_call_target="tpu_custom_call" | custom-call | bytes 67108864 | tf_op jit(solution)/shard_map/z_scan_1/pallas_call | solution.py:332
  300.8 30.2 %all_to_all.53.refs_1_ = bf16[4,2048,128]{2,1,0:T(8,128)(2,1)} all-to-all(bf16[4,2048,128]{2,1,0:T(8,128)(2,1)} %bitcast.53), channel_id=1, replica_groups=mesh['seq'=8,'head'=4] {'head'}, dimensions={0} | all-to-all | bytes 4194304 | tf_op jit(solution)/shard_map/all_to_all | solution.py:344
  330.9 7.5 %tail.1 = bf16[2048,512]{1,0:T(8,128)(2,1)} custom-call(bf16[4,2048,128]{2,1,0:T(8,128)(2,1)} %copy-done, bf16[4,2048,128]{2,1,0:T(8,128)(2,1)} %all_to_all.53.refs_1_, bf16[4,256,512]{2,1,0:T(8,128)(2,1)} %copy-done.3), custom_call_target="tpu_custom_call" | custom-call | tf_op jit(solution)/shard_map/tail/pallas_call | solution.py:348
  (51 shorter events, 2.0 us)
Async XLA Ops:
  0.0 12.2 %copy-start.8 = (s32[8192]{0:T(1024)S(1)}, s32[8192]{0:T(1024)}, u32[]{:S(2)}) copy-start(s32[8192]{0:T(1024)} %param.18) | copy-start | bytes 98308
  0.0 18.9 %copy-start.6 = (f32[4,8192]{1,0:T(4,128)S(1)}, f32[4,8192]{1,0:T(4,128)}, u32[]{:S(2)}) copy-start(f32[4,8192]{1,0:T(4,128)} %param.17) | copy-start | bytes 393220
  4.3 16.2 %all-to-all-start.1 = ((f32[8,2,4]{2,1,0:T(2,128)}), f32[8,2,4]{2,1,0:T(2,128)S(1)}, u32[]{:S(2)}, u32[]{:S(2)}) async-start(f32[8,2,4]{2,1,0:T(2,128)} %broadcast_in_dim.134), calls=%async_computation.1 | async-start | bytes 16384 | tf_op jit(solution)/shard_map/all_to_all | solution.py:178
  20.5 19.0 %all-to-all-start = ((s32[8,1,1024]{2,1,0:T(1,128)}), s32[8,1,1024]{2,1,0:T(1,128)S(1)}, u32[]{:S(2)}, u32[]{:S(2)}) async-start(s32[8,1,1024]{2,1,0:T(1,128)} %broadcast_subtract_fusion), calls=%async_computation | async-start | bytes 65536 | tf_op jit(solution)/shard_map/all_to_all | solution.py:263
  29.3 17.9 %copy-start.5 = (bf16[256,512]{1,0:T(8,128)(2,1)S(1)}, bf16[256,512]{1,0:T(8,128)(2,1)}, u32[]{:S(2)}) copy-start(bf16[256,512]{1,0:T(8,128)(2,1)} %param.25) | copy-start | bytes 786436
  29.3 17.9 %copy-start.9 = (f32[256]{0:T(256)S(1)}, f32[256]{0:T(256)}, u32[]{:S(2)}) copy-start(f32[256]{0:T(256)} %param.24) | copy-start | bytes 3076
  39.5 22.1 %copy-start.4 = (s32[8,1,1024]{2,1,0:T(1,128)}, s32[8,1,1024]{2,1,0:T(1,128)S(1)}, u32[]{:S(2)}) copy-start(s32[8,1,1024]{2,1,0:T(1,128)S(1)} %all-to-all-done) | copy-start | bytes 98308
  41.2 19.4 %all-to-all-start.2 = ((bf16[8,128,256]{2,1,0:T(8,128)(2,1)}), bf16[8,128,256]{2,1,0:T(8,128)(2,1)S(1)}, u32[]{:S(2)}, u32[]{:S(2)}) async-start(bf16[8,128,256]{2,1,0:T(8,128)(2,1)} %broadcast_in_dim.140), calls=%async_computation.2 | async-start | bytes 1048576 | tf_op jit(solution)/shard_map/all_to_all | solution.py:178
  61.7 40.2 %all-to-all-start.4 = ((bf16[4,256,512]{2,1,0:T(8,128)(2,1)}), bf16[4,256,512]{2,1,0:T(8,128)(2,1)S(1)}, u32[]{:S(2)}, u32[]{:S(2)}) async-start(bf16[4,256,512]{2,1,0:T(8,128)(2,1)} %broadcast_in_dim.141), calls=%async_computation.4 | async-start | bytes 2097152 | tf_op jit(solution)/shard_map/all_to_all | solution.py:178
  101.9 1.0 copy-start.3
  101.9 5.3 %copy-start.7 = (f32[4,8192]{1,0:T(4,128)S(1)}, f32[4,8192]{1,0:T(4,128)}, u32[]{:S(2)}) copy-start(f32[4,8192]{1,0:T(4,128)} %param.22) | copy-start | bytes 393220
  102.9 52.7 %all-to-all-start.3 = ((bf16[8,1024,128]{2,1,0:T(8,128)(2,1)}), bf16[8,1024,128]{2,1,0:T(8,128)(2,1)S(1)}, u32[]{:S(2)}, u32[]{:S(2)}) async-start(bf16[8,1024,128]{2,1,0:T(8,128)(2,1)} %bitcast.49), calls=%async_computation.3 | async-start | bytes 4194304 | tf_op jit(solution)/shard_map/all_to_all | solution.py:313
  155.6 1.3 copy-start.2
  187.1 51.5 %all-to-all-start.7 = ((bf16[8,1024,128]{2,1,0:T(8,128)(2,1)}), bf16[8,1024,128]{2,1,0:T(8,128)(2,1)S(1)}, u32[]{:S(2)}, u32[]{:S(2)}) async-start(bf16[8,1024,128]{2,1,0:T(8,128)(2,1)} %bitcast.23), calls=%async_computation.7 | async-start | bytes 4194304 | tf_op jit(solution)/shard_map/all_to_all | solution.py:313
  238.6 1.3 copy-start.1
  270.1 30.7 %all-to-all-start.6 = ((bf16[4,2048,128]{2,1,0:T(8,128)(2,1)}), bf16[4,2048,128]{2,1,0:T(8,128)(2,1)S(1)}, u32[]{:S(2)}, u32[]{:S(2)}) async-start(bf16[4,2048,128]{2,1,0:T(8,128)(2,1)} %bitcast.52), calls=%async_computation.6 | async-start | bytes 4194304 | tf_op jit(solution)/shard_map/all_to_all | solution.py:344
  300.8 30.2 %copy-start = (bf16[4,2048,128]{2,1,0:T(8,128)(2,1)}, bf16[4,2048,128]{2,1,0:T(8,128)(2,1)S(1)}, u32[]{:S(2)}) copy-start(bf16[4,2048,128]{2,1,0:T(8,128)(2,1)S(1)} %all-to-all-done.6.refs_0_) | copy-start | bytes 6291460

commit v3 on v2

--- a/solution.py
+++ b/solution.py
@@ -9,6 +9,7 @@
 from jax.sharding import PartitionSpec as P
 
 CHUNK = 256
+PAIR = 2
 STEP = 1024
 UNROLL = 32
 VMEM = 56 * 1024 * 1024
@@ -97,6 +98,26 @@
         b, contrib, (((0,), (0,)), ((), ())), preferred_element_type=jnp.float32
     )
     return y
+
+
+def pair_result(heads, first, mine, u_ref, b_ref, c_ref, col_ref, row_ref, state):
+    results = []
+    for j in range(PAIR):
+        at = slice(j * CHUNK, (j + 1) * CHUNK)
+        results.append(
+            chunk_result(
+                heads,
+                first,
+                mine,
+                u_ref[at, :],
+                b_ref[at, :],
+                c_ref[at, :],
+                col_ref[at, :],
+                row_ref[j],
+                state,
+            )
+        )
+    return results
 
 
 def scan_gather_kernel(
@@ -121,10 +142,10 @@
     def _():
         state[...] = start_ref[...]
 
-    y = chunk_result(
-        heads, first, mine, u_ref[...], b_ref[...], c_ref[...], col_ref[...], row_ref[0], state
-    )
-    held[pl.ds(pl.multiple_of(step * CHUNK, CHUNK), CHUNK), :] = y
+    results = pair_result(heads, first, mine, u_ref, b_ref, c_ref, col_ref, row_ref, state)
+    for j, y in enumerate(results):
+        base = pl.multiple_of((step * PAIR + j) * CHUNK, CHUNK)
+        held[pl.ds(base, CHUNK), :] = y
 
     @pl.when(step == pl.num_programs(0) - 1)
     def _():
@@ -145,11 +166,11 @@
     def _():
         state[...] = start_ref[...]
 
-    y = chunk_result(
-        heads, first, mine, u_ref[...], b_ref[...], c_ref[...], col_ref[...], row_ref[0], state
-    )
-    gate = gate_ref[...].astype(jnp.float32)
-    out_ref[...] = (y * gate / (1.0 + jnp.exp(-gate))).astype(out_ref.dtype)
+    results = pair_result(heads, first, mine, u_ref, b_ref, c_ref, col_ref, row_ref, state)
+    for j, y in enumerate(results):
+        at = slice(j * CHUNK, (j + 1) * CHUNK)
+        gate = gate_ref[at, :].astype(jnp.float32)
+        out_ref[at, :] = (y * gate / (1.0 + jnp.exp(-gate))).astype(out_ref.dtype)
 
 
 def tail_kernel(parts, *refs):
@@ -274,14 +295,14 @@
     cols = x_cols.shape[1]
     moved = 64 * count * part
 
-    def chunk_specs(u_at):
+    def chunk_specs(u_at, at):
         return [
-            by_row(CHUNK, part, u_at),
-            by_row(CHUNK, state),
-            by_row(CHUNK, state),
-            by_row(CHUNK, cols),
-            pl.BlockSpec((1, heads, CHUNK), lambda i: (i, 0, 0)),
-            pl.BlockSpec((state, part), lambda i: (0, u_at)),
+            by_row(PAIR * CHUNK, part, u_at),
+            by_row(PAIR * CHUNK, state),
+            by_row(PAIR * CHUNK, state),
+            by_row(PAIR * CHUNK, cols),
+            pl.BlockSpec((PAIR, heads, CHUNK), lambda i: (i, 0, 0)),
+            pl.BlockSpec((state, part), lambda i: (0, at)),
         ]
 
     x_final = pl.pallas_call(
@@ -301,8 +322,8 @@
         sent = pl.pallas_call(
             functools.partial(scan_gather_kernel, heads, p * own, own),
             out_shape=bf16(count, part),
-            grid=(count // CHUNK,),
-            in_specs=[smem()] + chunk_specs(p),
+            grid=(count // (PAIR * CHUNK),),
+            in_specs=[smem()] + chunk_specs(p, p),
             out_specs=whole(count, part),
             scratch_shapes=[f32(state, part), f32(count, part), f32(UNROLL, part)],
             compiler_params=params(),
@@ -313,7 +334,7 @@
         received.append(lax.all_to_all(sent.reshape(peers, share, part), "seq", 0, 0))
 
     mine = count // groups
-    swapped = []
+    finals, inputs = [], []
     done.append(weight)
     for p in range(parts):
         arrived = after(received[p], *done).reshape(count, part)
@@ -328,18 +349,23 @@
             cost_estimate=cost(0, moved // 2),
             name="z_place_%d" % p,
         )(place, arrived, z_in_proj, z_cols)
-        z_start = start_state(z_final, totals[:, 1, p * own : (p + 1) * own], part)
+        finals.append(z_final)
+        inputs.append(u_z)
+
+    z_start = start_state(jnp.concatenate(finals, axis=1), totals[:, 1], width)
+    swapped, done = [], []
+    for p in range(parts):
         gated = pl.pallas_call(
             functools.partial(scan_gate_kernel, heads, p * own, own),
             out_shape=bf16(count, part),
-            grid=(count // CHUNK,),
-            in_specs=chunk_specs(0) + [by_row(CHUNK, part, p)],
-            out_specs=by_row(CHUNK, part),
+            grid=(count // (PAIR * CHUNK),),
+            in_specs=chunk_specs(0, p) + [by_row(PAIR * CHUNK, part, p)],
+            out_specs=by_row(PAIR * CHUNK, part),
             scratch_shapes=[f32(state, part)],
             compiler_params=params(),
             cost_estimate=cost(0, moved),
             name="z_scan_%d" % p,
-        )(u_z, z_in_proj, z_out_proj, z_cols, z_rows, z_start, gate_branch)
+        )(inputs[p], z_in_proj, z_out_proj, z_cols, z_rows, after(z_start, *done), gate_branch)
         done = [gated]
         swapped.append(lax.all_to_all(gated.reshape(groups, mine, part), "head", 0, 0))
 

time: 342 us -> 342 us (level)
  waiting for transfers between devices: 42.8 us -> 102 us
  Pallas kernels: 175 us -> 139 us
  blocking collectives: 55.2 us -> 30.1 us
  starting transfers between devices: 33.8 us -> 38.1 us
    all_to_all x2, waiting for transfers between devices: 29.5 us -> 66.5 us  [body(): lax.all_to_all(sent.reshape(peers, share, part), 'seq', 0, 0)]
    all_to_all x2 -> x0, blocking collectives: 25 us -> none  [to_all(): lax.all_to_all(jnp.broadcast_to(value, (count,) + value.shape), axis, 0, 0)]
    pallas_call x2, Pallas kernels: 71 us -> 52.8 us  [body(): pl.pallas_call(functools.partial(scan_gather_kernel, heads, p * own, own)...]
    pallas_call x2, Pallas kernels: 52.3 us -> 34.6 us  [body(): pl.pallas_call(functools.partial(scan_gate_kernel, heads, p * own, own),...]
    all_to_all x3 -> x4, waiting for transfers between devices: 13.2 us -> 27.6 us  [to_all(): lax.all_to_all(jnp.broadcast_to(value, (count,) + value.shape), axis, 0, 0)]
    all_to_all x1, waiting for transfers between devices: 0.01 us -> 8.36 us  [body(): lax.all_to_all(gated.reshape(groups, mine, part), 'head', 0, 0)]
    all_to_all x3 -> x4, starting transfers between devices: 16.8 us -> 20.4 us  [to_all(): lax.all_to_all(jnp.broadcast_to(value, (count,) + value.shape), axis, 0, 0)]
  transfers between devices with their start and end apart: 7 -> 8, of which waited for: 3 -> 5; matrix products, arithmetic and copies ran while one was open for 6% -> 5% of each run, Pallas kernels for 39% -> 24%
where the time goes in v3:
time: 342 us; the launch traced here: 339 us
  Pallas kernels  139 us (41%)
  waiting for transfers between devices  102 us (30%)
  starting transfers between devices  38.1 us (11%)
  blocking collectives  30.1 us (9%)
  other arithmetic  14.8 us (4%)
  local copies, waits for them, and re-layouts  13.8 us (4%)
    all_to_all x2, waiting for transfers between devices, body(): lax.all_to_all(sent.reshape(peers, share, part), 'seq', 0, 0)  66.5 us
    pallas_call x2, Pallas kernels, body(): pl.pallas_call(functools.partial(scan_gather_kernel, heads, p * own, own)...  52.8 us
    pallas_call x2, Pallas kernels, body(): pl.pallas_call(functools.partial(scan_gate_kernel, heads, p * own, own),...  34.6 us
    pallas_call x2, Pallas kernels, body(): pl.pallas_call(functools.partial(place_kernel, heads, p * own, own), out_...  33.8 us
    all_to_all x1, blocking collectives, body(): lax.all_to_all(gated.reshape(groups, mine, part), 'head', 0, 0)  30.1 us
    all_to_all x4, waiting for transfers between devices, to_all(): lax.all_to_all(jnp.broadcast_to(value, (count,) + value.shape), axis, 0, 0)  27.6 us
    all_to_all x4, starting transfers between devices, to_all(): lax.all_to_all(jnp.broadcast_to(value, (count,) + value.shape), axis, 0, 0)  20.4 us
    pallas_call x1, Pallas kernels, body(): pl.pallas_call(functools.partial(final_kernel, heads, 0, heads), out_shap...  10.2 us
  transfers between devices with their start and end apart: 8, of which 5 were waited for; matrix products, arithmetic and copies ran while one was open for 5% of the time, Pallas kernels for 24%

profile of v3, /device:TPU:0, one launch (start us, length us, event | category | flops | bytes accessed | tf_op | source)
XLA Modules:
  0.0 339.2 jit_solution(6959429086976162495)
XLA Ops:
  0.0 1.0 broadcast_multiply_fusion.1
  1.0 0.4 fusion.2
  1.4 0.9 broadcast_multiply_fusion
  2.4 0.4 fusion
  2.9 0.3 reduce_window_sum.17
  3.2 0.3 reduce_window_sum.16
  3.5 0.2 slice_subtract_fusion
  3.7 0.6 broadcast_in_dim.89
  4.3 7.3 %all-to-all-start.1 = ((f32[8,2,4]{2,1,0:T(2,128)}), f32[8,2,4]{2,1,0:T(2,128)S(1)}, u32[]{:S(2)}, u32[]{:S(2)}) async-start(f32[8,2,4]{2,1,0:T(2,128)} %broadcast_in_dim.89), calls=%async_computation.1 | async-start | bytes 16384 | tf_op jit(solution)/shard_map/all_to_all | solution.py:199
  11.6 0.3 copy.106
  11.9 0.3 copy.107
  12.2 6.8 %sort.15 = (s32[8192]{0:T(1024)S(1)}, s32[8192]{0:T(1024)}) sort(s32[8192]{0:T(1024)S(1)} %copy-done.7, s32[8192]{0:T(1024)S(1)} %iota.51), dimensions={0}, to_apply=%region_0.0 | sort | flops 106496 | bytes 131072 | tf_op jit(solution)/shard_map/sort | solution.py:282
  19.0 0.9 exponential_multiply_fusion.3
  19.9 0.7 broadcast_subtract_fusion
  20.6 6.0 %all-to-all-start = ((s32[8,1,1024]{2,1,0:T(1,128)}), s32[8,1,1024]{2,1,0:T(1,128)S(1)}, u32[]{:S(2)}, u32[]{:S(2)}) async-start(s32[8,1,1024]{2,1,0:T(1,128)} %broadcast_subtract_fusion), calls=%async_computation | async-start | bytes 65536 | tf_op jit(solution)/shard_map/all_to_all | solution.py:284
  26.7 2.6 copy.108
  29.3 10.2 %x_final.1 = bf16[128,256]{1,0:T(8,128)(2,1)} custom-call(bf16[8192,256]{1,0:T(8,128)(2,1)} %u_ref.5, bf16[8192,128]{1,0:T(8,128)(2,1)} %b_ref.9, f32[8192,16]{1,0:T(8,128)} %bitcast.45), custom_call_target="tpu_custom_call" | custom-call | tf_op jit(solution)/shard_map/x_final/pallas_call | solution.py:308
  39.5 1.7 broadcast_in_dim.95
  41.2 6.0 %all-to-all-start.2 = ((bf16[8,128,256]{2,1,0:T(8,128)(2,1)}), bf16[8,128,256]{2,1,0:T(8,128)(2,1)S(1)}, u32[]{:S(2)}, u32[]{:S(2)}) async-start(bf16[8,128,256]{2,1,0:T(8,128)(2,1)} %broadcast_in_dim.95), calls=%async_computation.2 | async-start | bytes 1048576 | tf_op jit(solution)/shard_map/all_to_all | solution.py:199
  47.3 13.2 %all-to-all-done.2 = bf16[8,128,256]{2,1,0:T(8,128)(2,1)S(1)} async-done(((bf16[8,128,256]{2,1,0:T(8,128)(2,1)}), bf16[8,128,256]{2,1,0:T(8,128)(2,1)S(1)}, u32[]{:S(2)}, u32[]{:S(2)}) %all-to-all-start.2) | async-done | bytes 524320 | tf_op jit(solution)/shard_map/all_to_all | solution.py:199
  60.6 1.1 broadcast_in_dim.96
  61.6 3.5 %all-to-all-start.4 = ((bf16[4,256,512]{2,1,0:T(8,128)(2,1)}), bf16[4,256,512]{2,1,0:T(8,128)(2,1)S(1)}, u32[]{:S(2)}, u32[]{:S(2)}) async-start(bf16[4,256,512]{2,1,0:T(8,128)(2,1)} %broadcast_in_dim.96), calls=%async_computation.4 | async-start | bytes 2097152 | tf_op jit(solution)/shard_map/all_to_all | solution.py:199
  65.7 0.8 multiply_reduce_fusion.1.start_ref
  66.5 26.4 %x_scan_0.1 = bf16[8192,128]{1,0:T(8,128)(2,1)} custom-call(s32[8192]{0:T(1024)} %bitcast.53, bf16[8192,256]{1,0:T(8,128)(2,1)} %u_ref.5, bf16[8192,128]{1,0:T(8,128)(2,1)} %b_ref.9, bf16[8192,128]{1,0:T(8,128)(2,1)} %c_ref.5, f32[8192,16]{1,0:T(8,128)} %bitcast.46, f32[32,4,256]{2,1,0:T(4,128)} %get-tuple-element.32.row_ref, ...), custom_call_target="tpu_custom_call" | custom-call | bytes 67108864 | tf_op jit(solution)/shard_map/x_scan_0/pallas_call | solution.py:322
  92.9 1.0 copy-done.2
  93.9 3.7 %all-to-all-start.3 = ((bf16[8,1024,128]{2,1,0:T(8,128)(2,1)}), bf16[8,1024,128]{2,1,0:T(8,128)(2,1)S(1)}, u32[]{:S(2)}, u32[]{:S(2)}) async-start(bf16[8,1024,128]{2,1,0:T(8,128)(2,1)} %bitcast.49), calls=%async_computation.3 | async-start | bytes 4194304 | tf_op jit(solution)/shard_map/all_to_all | solution.py:334
  97.6 26.4 %x_scan_1.1 = bf16[8192,128]{1,0:T(8,128)(2,1)} custom-call(s32[8192]{0:T(1024)} %bitcast.54, bf16[8192,256]{1,0:T(8,128)(2,1)} %u_ref.5, bf16[8192,128]{1,0:T(8,128)(2,1)} %b_ref.9, bf16[8192,128]{1,0:T(8,128)(2,1)} %c_ref.5, f32[8192,16]{1,0:T(8,128)} %bitcast.47, f32[32,4,256]{2,1,0:T(4,128)} %get-tuple-element.32.row_ref, ...), custom_call_target="tpu_custom_call" | custom-call | bytes 67108864 | tf_op jit(solution)/shard_map/x_scan_1/pallas_call | solution.py:322
  124.0 22.6 %all-to-all-done.3 = bf16[8,1024,128]{2,1,0:T(8,128)(2,1)S(1)} async-done(((bf16[8,1024,128]{2,1,0:T(8,128)(2,1)}), bf16[8,1024,128]{2,1,0:T(8,128)(2,1)S(1)}, u32[]{:S(2)}, u32[]{:S(2)}) %all-to-all-start.3) | async-done | bytes 2097184 | tf_op jit(solution)/shard_map/all_to_all | solution.py:334
  146.6 1.3 copy-done.1
  147.9 4.4 %all-to-all-start.5 = ((bf16[8,1024,128]{2,1,0:T(8,128)(2,1)}), bf16[8,1024,128]{2,1,0:T(8,128)(2,1)}, u32[]{:S(2)}, u32[]{:S(2)}) async-start(bf16[8,1024,128]{2,1,0:T(8,128)(2,1)} %bitcast.48), calls=%async_computation.5 | async-start | bytes 4194304 | tf_op jit(solution)/shard_map/all_to_all | solution.py:334
  152.3 0.3 copy.110
  152.6 0.3 copy.111
  152.9 0.9 exponential_multiply_fusion.1
  153.9 2.6 copy.112
  156.5 43.9 %all-to-all-done.5 = bf16[8,1024,128]{2,1,0:T(8,128)(2,1)} async-done(((bf16[8,1024,128]{2,1,0:T(8,128)(2,1)}), bf16[8,1024,128]{2,1,0:T(8,128)(2,1)}, u32[]{:S(2)}, u32[]{:S(2)}) %all-to-all-start.5) | async-done | bytes 2097184 | tf_op jit(solution)/shard_map/all_to_all | solution.py:334
  200.4 16.9 %z_place_0.1 = (bf16[128,128]{1,0:T(8,128)(2,1)}, bf16[8192,128]{1,0:T(8,128)(2,1)}) custom-call(s32[8192]{0:T(1024)} %get-tuple-element.15.place_ref, bf16[8192,128]{1,0:T(8,128)(2,1)} %bitcast.50, bf16[8192,128]{1,0:T(8,128)(2,1)} %b_ref.13, f32[8192,16]{1,0:T(8,128)} %bitcast.41), custom_call_target="tpu_custom_call" | custom-call | bytes 33554432 | tf_op jit(solution)/shard_map/z_place_0/pallas_call | solution.py:341
  217.3 16.9 %z_place_1.1 = (bf16[128,128]{1,0:T(8,128)(2,1)}, bf16[8192,128]{1,0:T(8,128)(2,1)}) custom-call(s32[8192]{0:T(1024)} %get-tuple-element.15.place_ref, bf16[8192,128]{1,0:T(8,128)(2,1)} %bitcast.23.recv_ref, bf16[8192,128]{1,0:T(8,128)(2,1)} %b_ref.13, f32[8192,16]{1,0:T(8,128)} %bitcast.42), custom_call_target="tpu_custom_call" | custom-call | bytes 33554432 | tf_op jit(solution)/shard_map/z_place_1/pallas_call | solution.py:341
  234.2 0.8 pad_maximum_fusion.2
  235.0 0.8 broadcast_in_dim.100
  235.8 3.7 %all-to-all-start.6 = ((bf16[8,128,256]{2,1,0:T(8,128)(2,1)}), bf16[8,128,256]{2,1,0:T(8,128)(2,1)S(1)}, u32[]{:S(2)}, u32[]{:S(2)}) async-start(bf16[8,128,256]{2,1,0:T(8,128)(2,1)} %broadcast_in_dim.100), calls=%async_computation.6 | async-start | bytes 1048576 | tf_op jit(solution)/shard_map/all_to_all | solution.py:199
  239.8 14.4 %all-to-all-done.6 = bf16[8,128,256]{2,1,0:T(8,128)(2,1)S(1)} async-done(((bf16[8,128,256]{2,1,0:T(8,128)(2,1)}), bf16[8,128,256]{2,1,0:T(8,128)(2,1)S(1)}, u32[]{:S(2)}, u32[]{:S(2)}) %all-to-all-start.6) | async-done | bytes 524320 | tf_op jit(solution)/shard_map/all_to_all | solution.py:199
  254.1 0.8 multiply_reduce_fusion.start_ref
  254.9 17.3 %z_scan_0.1 = bf16[8192,128]{1,0:T(8,128)(2,1)} custom-call(bf16[8192,128]{1,0:T(8,128)(2,1)} %get-tuple-element.19.u_ref, bf16[8192,128]{1,0:T(8,128)(2,1)} %b_ref.13, bf16[8192,128]{1,0:T(8,128)(2,1)} %c_ref.7, f32[8192,16]{1,0:T(8,128)} %bitcast.43, f32[32,4,256]{2,1,0:T(4,128)} %get-tuple-element.31.row_ref, f32[128,256]{1,0:T(8,128)} %multiply_reduce_fusion.start_ref, ...), custom_call_target="tpu_custom_call" | custom-call | bytes 67108864 | tf_op jit(solution)/shard_map/z_scan_0/pallas_call | solution.py:358
  272.2 3.6 %all-to-all-start.7 = ((bf16[4,2048,128]{2,1,0:T(8,128)(2,1)}), bf16[4,2048,128]{2,1,0:T(8,128)(2,1)S(1)}, u32[]{:S(2)}, u32[]{:S(2)}) async-start(bf16[4,2048,128]{2,1,0:T(8,128)(2,1)} %bitcast.51), calls=%async_computation.7 | async-start | bytes 4194304 | tf_op jit(solution)/shard_map/all_to_all | solution.py:370
  275.8 17.3 %z_scan_1.1 = bf16[8192,128]{1,0:T(8,128)(2,1)} custom-call(bf16[8192,128]{1,0:T(8,128)(2,1)} %get-tuple-element.23.u_ref, bf16[8192,128]{1,0:T(8,128)(2,1)} %b_ref.13, bf16[8192,128]{1,0:T(8,128)(2,1)} %c_ref.7, f32[8192,16]{1,0:T(8,128)} %bitcast.44, f32[32,4,256]{2,1,0:T(4,128)} %get-tuple-element.31.row_ref, f32[128,256]{1,0:T(8,128)} %multiply_reduce_fusion.start_ref, ...), custom_call_target="tpu_custom_call" | custom-call | bytes 67108864 | tf_op jit(solution)/shard_map/z_scan_1/pallas_call | solution.py:358
  293.1 8.4 %all-to-all-done.7.refs_0_ = bf16[4,2048,128]{2,1,0:T(8,128)(2,1)S(1)} async-done(((bf16[4,2048,128]{2,1,0:T(8,128)(2,1)}), bf16[4,2048,128]{2,1,0:T(8,128)(2,1)S(1)}, u32[]{:S(2)}, u32[]{:S(2)}) %all-to-all-start.7) | async-done | bytes 2097184 | tf_op jit(solution)/shard_map/all_to_all | solution.py:370
  301.5 30.1 %all_to_all.46.refs_1_ = bf16[4,2048,128]{2,1,0:T(8,128)(2,1)} all-to-all(bf16[4,2048,128]{2,1,0:T(8,128)(2,1)} %bitcast.52), channel_id=1, replica_groups=mesh['seq'=8,'head'=4] {'head'}, dimensions={0} | all-to-all | bytes 4194304 | tf_op jit(solution)/shard_map/all_to_all | solution.py:370
  331.6 7.6 %tail.1 = bf16[2048,512]{1,0:T(8,128)(2,1)} custom-call(bf16[4,2048,128]{2,1,0:T(8,128)(2,1)} %copy-done, bf16[4,2048,128]{2,1,0:T(8,128)(2,1)} %all_to_all.46.refs_1_, bf16[4,256,512]{2,1,0:T(8,128)(2,1)} %copy-done.2), custom_call_target="tpu_custom_call" | custom-call | tf_op jit(solution)/shard_map/tail/pallas_call | solution.py:374
  (43 shorter events, 1.3 us)
Async XLA Ops:
  0.0 12.2 %copy-start.7 = (s32[8192]{0:T(1024)S(1)}, s32[8192]{0:T(1024)}, u32[]{:S(2)}) copy-start(s32[8192]{0:T(1024)} %param.18) | copy-start | bytes 98308
  0.0 19.0 %copy-start.5 = (f32[4,8192]{1,0:T(4,128)S(1)}, f32[4,8192]{1,0:T(4,128)}, u32[]{:S(2)}) copy-start(f32[4,8192]{1,0:T(4,128)} %param.17) | copy-start | bytes 393220
  4.3 16.3 %all-to-all-start.1 = ((f32[8,2,4]{2,1,0:T(2,128)}), f32[8,2,4]{2,1,0:T(2,128)S(1)}, u32[]{:S(2)}, u32[]{:S(2)}) async-start(f32[8,2,4]{2,1,0:T(2,128)} %broadcast_in_dim.89), calls=%async_computation.1 | async-start | bytes 16384 | tf_op jit(solution)/shard_map/all_to_all | solution.py:199
  20.6 18.9 %all-to-all-start = ((s32[8,1,1024]{2,1,0:T(1,128)}), s32[8,1,1024]{2,1,0:T(1,128)S(1)}, u32[]{:S(2)}, u32[]{:S(2)}) async-start(s32[8,1,1024]{2,1,0:T(1,128)} %broadcast_subtract_fusion), calls=%async_computation | async-start | bytes 65536 | tf_op jit(solution)/shard_map/all_to_all | solution.py:284
  29.3 17.9 %copy-start.4 = (bf16[256,512]{1,0:T(8,128)(2,1)S(1)}, bf16[256,512]{1,0:T(8,128)(2,1)}, u32[]{:S(2)}) copy-start(bf16[256,512]{1,0:T(8,128)(2,1)} %param.25) | copy-start | bytes 786436
  29.3 17.9 %copy-start.9 = (f32[256]{0:T(256)S(1)}, f32[256]{0:T(256)}, u32[]{:S(2)}) copy-start(f32[256]{0:T(256)} %param.24) | copy-start | bytes 3076
  39.5 22.1 %copy-start.3 = (s32[8,1,1024]{2,1,0:T(1,128)}, s32[8,1,1024]{2,1,0:T(1,128)S(1)}, u32[]{:S(2)}) copy-start(s32[8,1,1024]{2,1,0:T(1,128)S(1)} %all-to-all-done) | copy-start | bytes 98308
  41.2 19.4 %all-to-all-start.2 = ((bf16[8,128,256]{2,1,0:T(8,128)(2,1)}), bf16[8,128,256]{2,1,0:T(8,128)(2,1)S(1)}, u32[]{:S(2)}, u32[]{:S(2)}) async-start(bf16[8,128,256]{2,1,0:T(8,128)(2,1)} %broadcast_in_dim.95), calls=%async_computation.2 | async-start | bytes 1048576 | tf_op jit(solution)/shard_map/all_to_all | solution.py:199
  61.6 31.2 %all-to-all-start.4 = ((bf16[4,256,512]{2,1,0:T(8,128)(2,1)}), bf16[4,256,512]{2,1,0:T(8,128)(2,1)S(1)}, u32[]{:S(2)}, u32[]{:S(2)}) async-start(bf16[4,256,512]{2,1,0:T(8,128)(2,1)} %broadcast_in_dim.96), calls=%async_computation.4 | async-start | bytes 2097152 | tf_op jit(solution)/shard_map/all_to_all | solution.py:199
  92.9 1.1 copy-start.2
  93.9 52.7 %all-to-all-start.3 = ((bf16[8,1024,128]{2,1,0:T(8,128)(2,1)}), bf16[8,1024,128]{2,1,0:T(8,128)(2,1)S(1)}, u32[]{:S(2)}, u32[]{:S(2)}) async-start(bf16[8,1024,128]{2,1,0:T(8,128)(2,1)} %bitcast.49), calls=%async_computation.3 | async-start | bytes 4194304 | tf_op jit(solution)/shard_map/all_to_all | solution.py:334
  146.6 1.3 copy-start.1
  146.6 6.3 %copy-start.6 = (f32[4,8192]{1,0:T(4,128)S(1)}, f32[4,8192]{1,0:T(4,128)}, u32[]{:S(2)}) copy-start(f32[4,8192]{1,0:T(4,128)} %param.22) | copy-start | bytes 393220
  147.9 52.5 %all-to-all-start.5 = ((bf16[8,1024,128]{2,1,0:T(8,128)(2,1)}), bf16[8,1024,128]{2,1,0:T(8,128)(2,1)}, u32[]{:S(2)}, u32[]{:S(2)}) async-start(bf16[8,1024,128]{2,1,0:T(8,128)(2,1)} %bitcast.48), calls=%async_computation.5 | async-start | bytes 4194304 | tf_op jit(solution)/shard_map/all_to_all | solution.py:334
  217.3 16.9 %copy-start.8 = (bf16[128,128]{1,0:T(8,128)(2,1)S(1)}, bf16[128,128]{1,0:T(8,128)(2,1)}, u32[]{:S(2)}) copy-start(bf16[128,128]{1,0:T(8,128)(2,1)} %get-tuple-element.20) | copy-start | bytes 98308
  235.8 18.3 %all-to-all-start.6 = ((bf16[8,128,256]{2,1,0:T(8,128)(2,1)}), bf16[8,128,256]{2,1,0:T(8,128)(2,1)S(1)}, u32[]{:S(2)}, u32[]{:S(2)}) async-start(bf16[8,128,256]{2,1,0:T(8,128)(2,1)} %broadcast_in_dim.100), calls=%async_computation.6 | async-start | bytes 1048576 | tf_op jit(solution)/shard_map/all_to_all | solution.py:199
  272.2 29.3 %all-to-all-start.7 = ((bf16[4,2048,128]{2,1,0:T(8,128)(2,1)}), bf16[4,2048,128]{2,1,0:T(8,128)(2,1)S(1)}, u32[]{:S(2)}, u32[]{:S(2)}) async-start(bf16[4,2048,128]{2,1,0:T(8,128)(2,1)} %bitcast.51), calls=%async_computation.7 | async-start | bytes 4194304 | tf_op jit(solution)/shard_map/all_to_all | solution.py:370
  301.5 30.1 %copy-start = (bf16[4,2048,128]{2,1,0:T(8,128)(2,1)}, bf16[4,2048,128]{2,1,0:T(8,128)(2,1)S(1)}, u32[]{:S(2)}) copy-start(bf16[4,2048,128]{2,1,0:T(8,128)(2,1)S(1)} %all-to-all-done.7.refs_0_) | copy-start | bytes 6291460
